TPU v7x, 32 devices: a whole 2x2x4 slice. The times are simulated.
32 devices in a mesh: blade: 16 (over z, y, x), inst: 2 (over core).
Axes of the slice: x: 2, y: 2, z: 4, core: 2. Of those that a mesh axis runs over, the one named last changes fastest.
Arguments:
- tangent_seed: float32 [16, 5, 24, 1024], P('blade', None, 'inst'), may hold values from -6 to 6
- adjoint_seed: float32 [16, 5, 24, 1024], P('blade', None, 'inst'), may hold values from -6 to 6
- jacobian: bfloat16 [16, 24, 25, 1024], P('blade', 'inst'), may hold values from -1 to 4
- precond: bfloat16 [16, 24, 25, 1024], P('blade', 'inst'), may hold values from -1 to 4
- upwind: float32 [16, 1024], P('blade'), may hold values from 0.2 to 1
- up_weight: float32 [16, 256], P('blade'), may hold values from 0.3 to 1.2
- bottom_face_strength: float32 [16, 256], P('blade'), may hold values from 0.3 to 1.2
- up_cells: int32 [256], replicated, may hold values from 0 to 1023, as said below
- lo_cells: int32 [256], replicated, may hold values from 0 to 1023, as said below
- phase_index: int32 [11], replicated, may hold values from 0 to 15
Outputs:
- tangent_out: float32 [16, 5, 24, 1024], P('blade', None, 'inst')
- adjoint_out: float32 [16, 5, 24, 1024], P('blade', None, 'inst')
Inputs may be any that keep to these rules, and one draw needn't show every extreme that they name: `up_cells`: entry f of the table is one of the cells 4 f to 4 f + 3. `lo_cells`: entry f of the table is one of the cells 4 f to 4 f + 3.
All inputs are finite; a program needn't handle non-finite values.
Results may differ from a plain program's by a relative error of at most 0.0003.
Values sent between devices are 32-bit elements; how exact they have to be, the bound alone decides.
A program may use at most 64 MiB of HBM per device.

v0:
```python
import jax
import jax.numpy as jnp
from jax import lax
from jax.sharding import PartitionSpec as P

SNAPSHOT_COUNT = 24
NH = 11


OMEGA = 0.15


def passed_along(block, axis, distance):
    devices = range(lax.axis_size(axis))
    route = [((i - distance) % len(devices), i) for i in devices]
    return lax.ppermute(block, axis, route)


def spectral(phase_index, passages):
    sampled_moments = jnp.arange(SNAPSHOT_COUNT, dtype=jnp.int32)
    snapshot_displacement = sampled_moments[:, None] - sampled_moments[None, :]
    orders = jnp.arange(1, NH + 1, dtype=jnp.int32)
    wrapped = (
        jnp.mod(orders[:, None, None] * snapshot_displacement[None, :, :], SNAPSHOT_COUNT).astype(
            jnp.float32
        )
        / SNAPSHOT_COUNT
    )
    weights = orders.astype(jnp.float32)[:, None, None]
    skewed = -(2.0 / SNAPSHOT_COUNT) * jnp.sum(weights * jnp.sin(2.0 * jnp.pi * wrapped), axis=0)
    derivative = 0.5 * skewed - 0.5 * skewed.T
    phase_angle = phase_index.astype(jnp.float32)[:, None, None] / passages
    parity = 1.0 - 2.0 * jnp.mod(snapshot_displacement, 2).astype(jnp.float32)
    rotation = (1.0 + parity) / SNAPSHOT_COUNT + 2.0 / SNAPSHOT_COUNT * jnp.sum(
        jnp.cos(2.0 * jnp.pi * (wrapped - phase_angle)), axis=0
    )
    return (derivative, rotation)


def block_apply(blocks, vector):
    variables = vector.shape[1]
    result_rows = []
    for row_index in range(variables):
        summed = blocks[:, :, row_index * variables, :] * vector[:, 0]
        for column_index in range(1, variables):
            summed = (
                summed
                + blocks[:, :, row_index * variables + column_index, :] * vector[:, column_index]
            )
        result_rows.append(summed)
    return jnp.stack(result_rows, axis=1)


def block_apply_t(blocks, vector):
    variables = vector.shape[1]
    result_rows = []
    for column_index in range(variables):
        summed = blocks[:, :, column_index, :] * vector[:, 0]
        for row_index in range(1, variables):
            summed = (
                summed
                + blocks[:, :, row_index * variables + column_index, :] * vector[:, row_index]
            )
        result_rows.append(summed)
    return jnp.stack(result_rows, axis=1)


def instance_mix(matrix, vector):
    return jnp.einsum("ts,pvsc->pvtc", matrix, vector, precision=lax.Precision.HIGHEST)


def cell_mask(cells_table):
    face_count = cells_table.shape[0]
    within = cells_table - 4 * jnp.arange(face_count, dtype=jnp.int32)
    spread = jnp.repeat(within, 4)
    slot_in_group = jnp.mod(jnp.arange(4 * face_count, dtype=jnp.int32), 4)
    return (spread == slot_in_group).astype(jnp.float32)


def face_pick(vector, mask):
    lead = vector.shape[:-1]
    picked = (vector * mask).reshape(lead + (vector.shape[-1] // 4, 4))
    return jnp.sum(picked, axis=-1)


def face_spread(values, mask):
    return jnp.repeat(values, 4, axis=-1) * mask


def regroup(vector, lo_mask, up_mask, derivative, rotation):
    lo_face = face_pick(vector, lo_mask)
    up_face = face_pick(vector, up_mask)
    own_count = vector.shape[2]
    first_row = lax.axis_index("inst") * own_count
    own_deriv = lax.dynamic_slice_in_dim(derivative, first_row, own_count, 0)
    own_rot = lax.dynamic_slice_in_dim(rotation, first_row, own_count, 0)
    own_rot_t = lax.dynamic_slice_in_dim(rotation.T, first_row, own_count, 0)
    return (
        instance_mix(own_deriv, lax.all_gather(vector, "inst", axis=2, tiled=True)),
        instance_mix(own_rot, lax.all_gather(lo_face, "inst", axis=2, tiled=True)),
        instance_mix(own_rot_t, lax.all_gather(up_face, "inst", axis=2, tiled=True)),
    )


def cycle_faces(next_source, previous_source_term):
    from_next = jnp.concatenate([next_source[1:], passed_along(next_source, "blade", -1)], axis=0)
    from_prev = jnp.concatenate(
        [passed_along(previous_source_term, "blade", 1), previous_source_term[:-1]], axis=0
    )
    return (from_next, from_prev)


def on_device(
    tangent_seed,
    adjoint_seed,
    jacobian,
    precond,
    upwind,
    up_weight,
    bottom_face_strength,
    up_cells,
    lo_cells,
    phase_index,
):
    passages = tangent_seed.shape[0] * lax.axis_size("blade")
    derivative, rotation = spectral(phase_index, passages)
    up_mask = cell_mask(up_cells)
    lo_mask = cell_mask(lo_cells)
    dual_field = block_apply_t(precond, adjoint_seed)
    negated = -dual_field
    up_scale = up_weight[:, None, None, :]
    lo_scale = bottom_face_strength[:, None, None, :]
    timed_tan, lo_tan, up_tan = regroup(tangent_seed, lo_mask, up_mask, derivative, rotation)
    next_tan, previous_tangent = cycle_faces(lo_tan, up_tan)
    timed_adj, lo_adj, up_adj = regroup(negated, lo_mask, up_mask, derivative, rotation)
    next_adj, prev_adj = cycle_faces(-lo_scale * lo_adj, -up_scale * up_adj)
    shifted = jnp.pad(tangent_seed[..., :-1], ((0, 0), (0, 0), (0, 0), (1, 0)))
    applied = (
        block_apply(jacobian, tangent_seed) - upwind[:, None, None, :] * shifted + OMEGA * timed_tan
    )
    applied = (
        applied
        - face_spread(up_scale * next_tan, up_mask)
        - face_spread(lo_scale * previous_tangent, lo_mask)
    )
    tangent_out = block_apply(precond, applied)
    shifted = jnp.pad(
        (upwind[:, None, None, :] * dual_field)[..., 1:], ((0, 0), (0, 0), (0, 0), (0, 1))
    )
    adjoint_out = block_apply_t(jacobian, dual_field) - shifted + OMEGA * timed_adj
    adjoint_out = adjoint_out - face_spread(prev_adj, lo_mask) - face_spread(next_adj, up_mask)
    return (tangent_out, adjoint_out)


def solution(mesh):
    in_specs = (
        P("blade", None, "inst", None),
        P("blade", None, "inst", None),
        P("blade", "inst", None, None),
        P("blade", "inst", None, None),
        P("blade", None),
        P("blade", None),
        P("blade", None),
        P(),
        P(),
        P(),
    )
    out_specs = (P("blade", None, "inst", None), P("blade", None, "inst", None))
    return jax.shard_map(
        on_device, mesh=mesh, in_specs=in_specs, out_specs=out_specs, check_vma=False
    )
```

profile of v0, /device:TPU:0, one launch (start us, length us, event | category | flops | bytes accessed | tf_op | source)
XLA Modules:
  0.0 91.7 jit_solution(63031265090719832)
XLA Ops:
  0.7 0.7 fusion.151
  1.6 0.7 fusion.150
  2.5 1.8 %fusion.170 = (f32[1,5,12,1024]{3,2,1,0:T(8,128)S(1)}, f32[1,5,12,1024]{3,2,1,0:T(8,128)S(1)}, f32[1,5,12,1024]{3,2,1,0:T(8,128)}) fusion(f32[1,5,12,1024]{3,0,2,1:T(1,128)} %param.10, f32[1024]{0:T(1024)S(1)} %get-tuple-element.88, f32[1024]{0:T(1024)S(1)} %get-tuple-element.89), kind=kLoop, calls=%fused_computation.354 | loop fusion | flops 122880 | bytes 991232 | tf_op args[0]
  4.3 1.7 %copy.312 = f32[1,5,12,1024]{2,3,1,0:T(8,128)S(1)} copy(f32[1,5,12,1024]{3,2,1,0:T(8,128)} %get-tuple-element.77) | data formatting | bytes 491520 | tf_op jit(solution)/shard_map/mul | solution.py:82
  6.0 2.9 %reduce_sum.66 = f32[5,12,256]{1,2,0:T(8,128)} reduce(f32[5,12,256,4]{1,3,2,0:T(4,128)S(1)} %bitcast.467, f32[]{:T(128)} %constant.66.clone.1), dimensions={3}, to_apply=%region_3.4 | reduce | flops 46080 | bytes 307204 | tf_op jit(solution)/shard_map/reduce_sum | solution.py:83
  8.9 1.4 %copy.313 = f32[5,12,256]{2,0,1:T(8,128)S(1)} copy(f32[5,12,256]{1,2,0:T(8,128)} %reduce_sum.66) | data formatting | bytes 122880 | tf_op jit(solution)/shard_map/reduce_sum | solution.py:83
  10.3 2.0 %all-gather.1 = f32[5,24,256]{2,0,1:T(8,128)S(1)} all-gather(f32[5,12,256]{2,0,1:T(8,128)S(1)} %copy.313), channel_id=3, replica_groups=mesh['blade'=16,'inst'=2] {'inst'}, dimensions={1}, use_global_device_ids=true | all-gather | bytes 184320 | tf_op jit(solution)/shard_map/all_gather | solution.py:101
  12.4 1.7 %multiply_reduce_fusion.2 = (f32[24,24]{1,0:T(8,128)}, f32[24,24]{1,0:T(8,128)S(1)}) fusion(s32[24,24]{1,0:T(8,128)S(1)} %iota_subtract_fusion, s32[11]{0:T(128)S(1)} %get-tuple-element.90, f32[11]{0:T(128)S(1)} %get-tuple-element.91, f32[11]{0:T(128)S(1)} %convert_multiply_fusion.75), kind=kLoop, calls=%fused_computation.31 | loop fusion | flops 93888 | bytes 7044 | tf_op jit(solution)/shard_map/reduce_sum | solution.py:30
  14.1 1.0 %convolution_bitcast_fusion.2 = f32[1,5,12,256]{3,2,1,0:T(8,128)} fusion(f32[5,24,256]{2,0,1:T(8,128)S(1)} %all-gather.1, f32[24,24]{1,0:T(8,128)S(1)} %fusion.131, s32[]{:T(128)S(6)} %select_n.47), kind=kOutput, calls=%fused_computation.14 | convolution fusion | flops 4423680 | bytes 186628 | tf_op jit(solution)/shard_map/ts,pvsc->pvtc/dot_general | solution.py:69
  15.0 2.8 %collective-permute-start.1 = (f32[1,5,12,256]{3,2,1,0:T(8,128)}, f32[1,5,12,256]{3,2,1,0:T(8,128)}, u32[]{:S(2)}, u32[]{:S(2)}) collective-permute-start(f32[1,5,12,256]{3,2,1,0:T(8,128)} %convolution_bitcast_fusion.2), channel_id=1, source_target_pairs={{30,0},{0,2},{2,4},{4,6},{6,8},{8,10},{10,12},{12,14},{14,16},{16,... | collective-permute-start | bytes 184328 | tf_op jit(solution)/shard_map/ppermute | solution.py:16
  17.9 0.8 copy.306
  18.7 2.9 %reduce_sum.63 = f32[5,12,256]{1,2,0:T(8,128)} reduce(f32[5,12,256,4]{1,3,2,0:T(4,128)S(1)} %bitcast.466, f32[]{:T(128)} %constant.66.clone.1), dimensions={3}, to_apply=%region_1.2 | reduce | flops 46080 | bytes 307204 | tf_op jit(solution)/shard_map/reduce_sum | solution.py:83
  21.5 1.5 %copy.307 = f32[5,12,256]{2,0,1:T(8,128)S(1)} copy(f32[5,12,256]{1,2,0:T(8,128)} %reduce_sum.63) | data formatting | bytes 122880 | tf_op jit(solution)/shard_map/reduce_sum | solution.py:83
  23.0 1.9 %all-gather = f32[5,24,256]{2,0,1:T(8,128)S(1)} all-gather(f32[5,12,256]{2,0,1:T(8,128)S(1)} %copy.307), channel_id=2, replica_groups=mesh['blade'=16,'inst'=2] {'inst'}, dimensions={1}, use_global_device_ids=true | all-gather | bytes 184320 | tf_op jit(solution)/shard_map/all_gather | solution.py:100
  25.0 0.9 convolution_bitcast_fusion.3
  25.9 4.0 %collective-permute-start = (f32[1,5,12,256]{3,2,1,0:T(8,128)}, f32[1,5,12,256]{3,2,1,0:T(8,128)}, u32[]{:S(2)}, u32[]{:S(2)}) collective-permute-start(f32[1,5,12,256]{3,2,1,0:T(8,128)} %convolution_bitcast_fusion.3), channel_id=1, source_target_pairs={{2,0},{4,2},{6,4},{8,6},{10,8},{12,10},{14,12},{16,14},{18,16},{20... | collective-permute-start | bytes 184328 | tf_op jit(solution)/shard_map/ppermute | solution.py:16
  29.9 2.1 %fusion.168 = (bf16[1,12,1,1024]{3,2,1,0:T(2,128)(2,1)S(1)}, bf16[1,12,1,1024]{3,2,1,0:T(2,128)(2,1)S(1)}, bf16[1,12,1,1024]{3,2,1,0:T(2,128)(2,1)S(1)}, bf16[1,...) fusion(bf16[1,12,25,1024]{3,2,1,0:T(8,128)(2,1)} %param.12), kind=kLoop, calls=%fused_computation.352 | loop fusion | bytes 294912 | tf_op jit(solution)/shard_map/slice | solution.py:44
  31.9 4.7 %fusion.167 = (bf16[1,12,1,1024]{3,2,1,0:T(2,128)(2,1)}, bf16[1,12,1,1024]{3,2,1,0:T(2,128)(2,1)}, bf16[1,12,1,1024]{3,2,1,0:T(2,128)(2,1)}, bf16[1,12,1,1024]{3...) fusion(bf16[1,12,25,1024]{3,2,1,0:T(8,128)(2,1)} %param.12), kind=kLoop, calls=%fused_computation.351 | loop fusion | bytes 933888 | tf_op jit(solution)/shard_map/slice | solution.py:48
  36.7 0.2 fusion.166
  37.0 1.0 %fusion.165 = (bf16[1,12,1,1024]{3,2,1,0:T(2,128)(2,1)S(1)}, bf16[1,12,1,1024]{3,2,1,0:T(2,128)(2,1)S(1)}, bf16[1,12,1,1024]{3,2,1,0:T(2,128)(2,1)S(1)}, bf16[1,...) fusion(bf16[1,12,25,1024]{3,2,1,0:T(8,128)(2,1)S(1)} %copy-done.1), kind=kLoop, calls=%fused_computation.349 | loop fusion | bytes 933888 | tf_op jit(solution)/shard_map/slice | solution.py:48
  38.4 0.9 fusion.40
  39.4 0.2 copy.349
  39.8 0.2 copy.350
  40.1 0.8 copy.355
  41.1 0.2 copy.351
  41.5 0.2 copy.352
  42.0 0.2 copy.353
  42.7 0.3 multiply_reduce_fusion.1
  43.1 2.1 %all-gather.3 = f32[5,24,256]{2,0,1:T(8,128)S(1)} all-gather(f32[5,12,256]{2,0,1:T(8,128)S(1)} %copy.368), channel_id=5, replica_groups=mesh['blade'=16,'inst'=2] {'inst'}, dimensions={1}, use_global_device_ids=true | all-gather | bytes 184320 | tf_op jit(solution)/shard_map/all_gather | solution.py:100
  45.2 0.9 fusion.11
  46.1 2.0 %collective-permute-start.3 = (f32[1,5,12,256]{3,2,1,0:T(8,128)}, f32[1,5,12,256]{3,2,1,0:T(8,128)}, u32[]{:S(2)}, u32[]{:S(2)}) collective-permute-start(f32[1,5,12,256]{3,2,1,0:T(8,128)} %fusion.11), channel_id=1, source_target_pairs={{2,0},{4,2},{6,4},{8,6},{10,8},{12,10},{14,12},{16,14},{18,16},{20... | collective-permute-start | bytes 184328 | tf_op jit(solution)/shard_map/ppermute | solution.py:16
  48.2 2.1 %all-gather.2 = f32[5,24,256]{2,0,1:T(8,128)S(1)} all-gather(f32[5,12,256]{2,0,1:T(8,128)S(1)} %copy.361), channel_id=4, replica_groups=mesh['blade'=16,'inst'=2] {'inst'}, dimensions={1}, use_global_device_ids=true | all-gather | bytes 184320 | tf_op jit(solution)/shard_map/all_gather | solution.py:101
  50.2 1.0 %fusion.9 = f32[1,5,12,256]{3,2,1,0:T(8,128)} fusion(f32[5,24,256]{2,0,1:T(8,128)S(1)} %all-gather.2, f32[256]{0:T(256)S(1)} %neg.43, f32[24,24]{1,0:T(8,128)S(1)} %fusion.131, s32[]{:T(128)S(6)} %select_n.47), kind=kOutput, calls=%fused_computation.13 | convolution fusion | flops 4439040 | bytes 187652 | tf_op jit(solution)/shard_map/ts,pvsc->pvtc/dot_general | solution.py:69
  51.3 2.2 %all_gather.18 = f32[1,5,24,1024]{3,0,1,2:T(1,128)S(1)} all-gather(f32[1,5,12,1024]{3,0,1,2:T(1,128)S(1)} %copy.303), channel_id=1, replica_groups=mesh['blade'=16,'inst'=2] {'inst'}, dimensions={2}, use_global_device_ids=true | all-gather | bytes 737280 | tf_op jit(solution)/shard_map/all_gather | solution.py:99
  53.4 0.8 copy.301
  54.2 0.6 fusion.159
  54.9 0.9 fusion.70
  55.8 0.9 fusion.75
  56.7 0.9 fusion.90
  57.7 0.9 fusion.80
  58.6 0.9 fusion.95
  59.7 0.6 copy-done.5
  60.3 0.3 copy.347
  60.6 2.5 %all_gather.21 = f32[1,5,24,1024]{3,0,1,2:T(1,128)} all-gather(f32[1,5,12,1024]{3,0,1,2:T(1,128)S(1)} %copy.347), channel_id=1, replica_groups=mesh['blade'=16,'inst'=2] {'inst'}, dimensions={2}, use_global_device_ids=true | all-gather | bytes 737280 | tf_op jit(solution)/shard_map/all_gather | solution.py:99
  63.2 0.9 slice_multiply_fusion
  64.2 0.9 multiply_bitcast_fusion
  65.1 1.1 %copy.316 = f32[5,12,256]{1,2,0:T(8,128)} copy(f32[5,12,256]{2,1,0:T(8,128)S(1)} %multiply_bitcast_fusion) | data formatting | bytes 122880 | tf_op jit(solution)/shard_map/mul | solution.py:144
  66.2 1.5 %broadcast_in_dim.48 = f32[5,12,256,4]{1,3,2,0:T(4,128)S(1)} broadcast(f32[5,12,256]{1,2,0:T(8,128)} %copy.316), dimensions={0,1,2} | broadcast | bytes 307200 | tf_op jit(solution)/shard_map/broadcast_in_dim | solution.py:87
  67.8 1.5 %copy.317 = f32[1,5,12,1024]{3,2,1,0:T(8,128)} copy(f32[1,5,12,1024]{2,3,1,0:T(8,128)S(1)} %bitcast.468) | data formatting | bytes 491520 | tf_op jit(solution)/shard_map/broadcast_in_dim | solution.py:87
  69.3 0.9 multiply_bitcast_fusion.1
  70.2 1.1 %copy.309 = f32[5,12,256]{1,2,0:T(8,128)} copy(f32[5,12,256]{2,1,0:T(8,128)S(1)} %multiply_bitcast_fusion.1) | data formatting | bytes 122880 | tf_op jit(solution)/shard_map/mul | solution.py:143
  71.3 1.5 %broadcast_in_dim.21 = f32[5,12,256,4]{1,3,2,0:T(4,128)S(1)} broadcast(f32[5,12,256]{1,2,0:T(8,128)} %copy.309), dimensions={0,1,2} | broadcast | bytes 307200 | tf_op jit(solution)/shard_map/broadcast_in_dim | solution.py:87
  72.9 1.5 %copy.310 = f32[1,5,12,1024]{3,2,1,0:T(8,128)} copy(f32[1,5,12,1024]{2,3,1,0:T(8,128)S(1)} %bitcast.469) | data formatting | bytes 491520 | tf_op jit(solution)/shard_map/broadcast_in_dim | solution.py:87
  74.5 1.9 %fusion.4 = f32[1,5,12,1024]{3,2,1,0:T(8,128)S(1)} fusion(f32[1,5,24,1024]{3,0,1,2:T(1,128)S(1)} %all_gather.18, f32[1,5,12,1024]{3,2,1,0:T(8,128)} %copy.317, f32[1,5,12,1024]{3,2,1,0:T(8,128)} %copy.310, f32[1,5,12,1024]{3,2,1,0:T(8,128)} %copy-done.5, f32[1,5,12,1023]{3,2,1,0:T(8,128)S(1)} %bitcast.465, f32[1024]{0:T(1024)S(1)} %get-tuple-element.89, ...), kind=kOutput, calls=%fused_computation.6 | convolution fusion | flops 18186528 | bytes 1987476 | tf_op jit(solution)/shard_map/ts,pvsc->pvtc/dot_general | solution.py:69
  76.5 1.0 %fusion.45 = f32[1,5,12,1024]{3,2,1,0:T(8,128)S(1)} fusion(f32[1,5,12,1024]{3,2,1,0:T(8,128)S(1)} %fusion.4, bf16[1,12,1,1024]{3,2,1,0:T(2,128)(2,1)} %copy-done.11, bf16[1,12,1,1024]{3,2,1,0:T(2,128)(2,1)} %copy-done.10, bf16[1,12,1,1024]{3,2,1,0:T(2,128)(2,1)} %copy-done.46, bf16[1,12,1,1024]{3,2,1,0:T(2,128)(2,1)} %copy-done.45, ...), kind=kLoop, calls=%fused_computation.164 | loop fusion | flops 172031 | bytes 434176
  77.9 0.9 %copy.372 = f32[1,5,12,1024]{3,0,2,1:T(1,128)} copy(f32[1,5,12,1024]{3,2,1,0:T(8,128)S(1)} %fusion.65) | data formatting | bytes 491520
  78.8 2.0 %copy.370 = f32[5,12,256]{1,2,0:T(8,128)} copy(f32[5,12,256]{2,1,0:T(8,128)} %bitcast.136) | data formatting | bytes 122880 | tf_op jit(solution)/shard_map/ppermute | solution.py:16
  80.8 1.5 %broadcast_in_dim.52 = f32[5,12,256,4]{1,3,2,0:T(4,128)S(1)} broadcast(f32[5,12,256]{1,2,0:T(8,128)} %copy.370), dimensions={0,1,2} | broadcast | bytes 307200 | tf_op jit(solution)/shard_map/broadcast_in_dim | solution.py:87
  82.4 1.5 %copy.371 = f32[1,5,12,1024]{3,2,1,0:T(8,128)} copy(f32[1,5,12,1024]{2,3,1,0:T(8,128)S(1)} %bitcast.470) | data formatting | bytes 491520 | tf_op jit(solution)/shard_map/broadcast_in_dim | solution.py:87
  83.9 2.0 %copy.364 = f32[5,12,256]{1,2,0:T(8,128)} copy(f32[5,12,256]{2,1,0:T(8,128)} %bitcast.132) | data formatting | bytes 122880 | tf_op jit(solution)/shard_map/ppermute | solution.py:16
  85.9 1.6 %broadcast_in_dim.50 = f32[5,12,256,4]{1,3,2,0:T(4,128)S(1)} broadcast(f32[5,12,256]{1,2,0:T(8,128)} %copy.364), dimensions={0,1,2} | broadcast | bytes 307200 | tf_op jit(solution)/shard_map/broadcast_in_dim | solution.py:87
  87.5 1.5 %copy.365 = f32[1,5,12,1024]{3,2,1,0:T(8,128)} copy(f32[1,5,12,1024]{2,3,1,0:T(8,128)S(1)} %bitcast.471) | data formatting | bytes 491520 | tf_op jit(solution)/shard_map/broadcast_in_dim | solution.py:87
  89.1 1.7 %fusion.7 = f32[1,5,12,1024]{3,2,1,0:T(8,128)S(1)} fusion(f32[1,5,24,1024]{3,0,1,2:T(1,128)S(1)} %copy-done, f32[1,5,12,1024]{3,2,1,0:T(8,128)} %copy.371, f32[1,5,12,1024]{3,2,1,0:T(8,128)} %copy.365, f32[1,5,12,1024]{3,2,1,0:T(8,128)} %copy-done.4, f32[1,5,12,1023]{3,2,1,0:T(8,128)S(1)} %copy-done.2, f32[1024]{0:T(1024)S(1)} %get-tuple-element.89, ...), kind=kOutput, calls=%fused_computation.9 | convolution fusion | flops 18125088 | bytes 1826820 | tf_op jit(solution)/shard_map/ts,pvsc->pvtc/dot_general | solution.py:69
  90.8 0.9 %copy.373 = f32[1,5,12,1024]{3,0,2,1:T(1,128)} copy(f32[1,5,12,1024]{3,2,1,0:T(8,128)S(1)} %fusion.7) | data formatting | bytes 491520
  (187 shorter events, 2.9 us)
Async XLA Ops:
  6.0 6.3 %copy-start.70 = (s32[11]{0:T(128)S(1)}, s32[11]{0:T(128)}, u32[]{:S(2)}) copy-start(s32[11]{0:T(128)} %param.19) | copy-start | bytes 136
  15.0 49.2 %collective-permute-start.1 = (f32[1,5,12,256]{3,2,1,0:T(8,128)}, f32[1,5,12,256]{3,2,1,0:T(8,128)}, u32[]{:S(2)}, u32[]{:S(2)}) collective-permute-start(f32[1,5,12,256]{3,2,1,0:T(8,128)} %convolution_bitcast_fusion.2), channel_id=1, source_target_pairs={{30,0},{0,2},{2,4},{4,6},{6,8},{8,10},{10,12},{12,14},{14,16},{16,... | collective-permute-start | bytes 184328 | tf_op jit(solution)/shard_map/ppermute | solution.py:16
  21.5 15.1 %copy-start.1 = (bf16[1,12,25,1024]{3,2,1,0:T(8,128)(2,1)S(1)}, bf16[1,12,25,1024]{3,2,1,0:T(8,128)(2,1)}, u32[]{:S(2)}) copy-start(bf16[1,12,25,1024]{3,2,1,0:T(8,128)(2,1)} %param.13) | copy-start | bytes 1843204
  25.9 12.5 %copy-start.63 = (f32[1,5,12,1024]{3,0,2,1:T(1,128)S(1)}, f32[1,5,12,1024]{3,0,2,1:T(1,128)}, u32[]{:S(2)}) copy-start(f32[1,5,12,1024]{3,0,2,1:T(1,128)} %param.11) | copy-start | bytes 737284
  25.9 43.4 %collective-permute-start = (f32[1,5,12,256]{3,2,1,0:T(8,128)}, f32[1,5,12,256]{3,2,1,0:T(8,128)}, u32[]{:S(2)}, u32[]{:S(2)}) collective-permute-start(f32[1,5,12,256]{3,2,1,0:T(8,128)} %convolution_bitcast_fusion.3), channel_id=1, source_target_pairs={{2,0},{4,2},{6,4},{8,6},{10,8},{12,10},{14,12},{16,14},{18,16},{20... | collective-permute-start | bytes 184328 | tf_op jit(solution)/shard_map/ppermute | solution.py:16
  38.0 2.9 %copy-start.12 = (bf16[1,12,1,1024]{3,2,1,0:T(2,128)(2,1)}, bf16[1,12,1,1024]{3,2,1,0:T(2,128)(2,1)S(1)}, u32[]{:S(2)}) copy-start(bf16[1,12,1,1024]{3,2,1,0:T(2,128)(2,1)S(1)} %get-tuple-element.20) | copy-start | bytes 73732
  38.0 2.9 %copy-start.14 = (bf16[1,12,1,1024]{3,2,1,0:T(2,128)(2,1)}, bf16[1,12,1,1024]{3,2,1,0:T(2,128)(2,1)S(1)}, u32[]{:S(2)}) copy-start(bf16[1,12,1,1024]{3,2,1,0:T(2,128)(2,1)S(1)} %get-tuple-element.25) | copy-start | bytes 73732
  38.0 2.9 %copy-start.16 = (bf16[1,12,1,1024]{3,2,1,0:T(2,128)(2,1)}, bf16[1,12,1,1024]{3,2,1,0:T(2,128)(2,1)S(1)}, u32[]{:S(2)}) copy-start(bf16[1,12,1,1024]{3,2,1,0:T(2,128)(2,1)S(1)} %get-tuple-element.30) | copy-start | bytes 73732
  38.0 2.9 %copy-start.18 = (bf16[1,12,1,1024]{3,2,1,0:T(2,128)(2,1)}, bf16[1,12,1,1024]{3,2,1,0:T(2,128)(2,1)S(1)}, u32[]{:S(2)}) copy-start(bf16[1,12,1,1024]{3,2,1,0:T(2,128)(2,1)S(1)} %get-tuple-element.35) | copy-start | bytes 73732
  38.0 2.9 %copy-start.20 = (bf16[1,12,1,1024]{3,2,1,0:T(2,128)(2,1)}, bf16[1,12,1,1024]{3,2,1,0:T(2,128)(2,1)S(1)}, u32[]{:S(2)}) copy-start(bf16[1,12,1,1024]{3,2,1,0:T(2,128)(2,1)S(1)} %get-tuple-element.21) | copy-start | bytes 73732
  38.0 2.9 %copy-start.22 = (bf16[1,12,1,1024]{3,2,1,0:T(2,128)(2,1)}, bf16[1,12,1,1024]{3,2,1,0:T(2,128)(2,1)S(1)}, u32[]{:S(2)}) copy-start(bf16[1,12,1,1024]{3,2,1,0:T(2,128)(2,1)S(1)} %get-tuple-element.26) | copy-start | bytes 73732
  38.0 2.9 %copy-start.24 = (bf16[1,12,1,1024]{3,2,1,0:T(2,128)(2,1)}, bf16[1,12,1,1024]{3,2,1,0:T(2,128)(2,1)S(1)}, u32[]{:S(2)}) copy-start(bf16[1,12,1,1024]{3,2,1,0:T(2,128)(2,1)S(1)} %get-tuple-element.31) | copy-start | bytes 73732
  38.0 2.9 %copy-start.26 = (bf16[1,12,1,1024]{3,2,1,0:T(2,128)(2,1)}, bf16[1,12,1,1024]{3,2,1,0:T(2,128)(2,1)S(1)}, u32[]{:S(2)}) copy-start(bf16[1,12,1,1024]{3,2,1,0:T(2,128)(2,1)S(1)} %get-tuple-element.36) | copy-start | bytes 73732
  38.0 2.9 %copy-start.28 = (bf16[1,12,1,1024]{3,2,1,0:T(2,128)(2,1)}, bf16[1,12,1,1024]{3,2,1,0:T(2,128)(2,1)S(1)}, u32[]{:S(2)}) copy-start(bf16[1,12,1,1024]{3,2,1,0:T(2,128)(2,1)S(1)} %get-tuple-element.22) | copy-start | bytes 73732
  38.0 2.9 %copy-start.30 = (bf16[1,12,1,1024]{3,2,1,0:T(2,128)(2,1)}, bf16[1,12,1,1024]{3,2,1,0:T(2,128)(2,1)S(1)}, u32[]{:S(2)}) copy-start(bf16[1,12,1,1024]{3,2,1,0:T(2,128)(2,1)S(1)} %get-tuple-element.27) | copy-start | bytes 73732
  38.1 2.9 %copy-start.32 = (bf16[1,12,1,1024]{3,2,1,0:T(2,128)(2,1)}, bf16[1,12,1,1024]{3,2,1,0:T(2,128)(2,1)S(1)}, u32[]{:S(2)}) copy-start(bf16[1,12,1,1024]{3,2,1,0:T(2,128)(2,1)S(1)} %get-tuple-element.32) | copy-start | bytes 73732
  38.1 2.9 %copy-start.34 = (bf16[1,12,1,1024]{3,2,1,0:T(2,128)(2,1)}, bf16[1,12,1,1024]{3,2,1,0:T(2,128)(2,1)S(1)}, u32[]{:S(2)}) copy-start(bf16[1,12,1,1024]{3,2,1,0:T(2,128)(2,1)S(1)} %get-tuple-element.37) | copy-start | bytes 73732
  38.1 2.9 %copy-start.36 = (bf16[1,12,1,1024]{3,2,1,0:T(2,128)(2,1)}, bf16[1,12,1,1024]{3,2,1,0:T(2,128)(2,1)S(1)}, u32[]{:S(2)}) copy-start(bf16[1,12,1,1024]{3,2,1,0:T(2,128)(2,1)S(1)} %get-tuple-element.23) | copy-start | bytes 73732
  38.1 2.9 %copy-start.38 = (bf16[1,12,1,1024]{3,2,1,0:T(2,128)(2,1)}, bf16[1,12,1,1024]{3,2,1,0:T(2,128)(2,1)S(1)}, u32[]{:S(2)}) copy-start(bf16[1,12,1,1024]{3,2,1,0:T(2,128)(2,1)S(1)} %get-tuple-element.28) | copy-start | bytes 73732
  38.1 2.9 %copy-start.40 = (bf16[1,12,1,1024]{3,2,1,0:T(2,128)(2,1)}, bf16[1,12,1,1024]{3,2,1,0:T(2,128)(2,1)S(1)}, u32[]{:S(2)}) copy-start(bf16[1,12,1,1024]{3,2,1,0:T(2,128)(2,1)S(1)} %get-tuple-element.33) | copy-start | bytes 73732
  38.1 2.9 %copy-start.42 = (bf16[1,12,1,1024]{3,2,1,0:T(2,128)(2,1)}, bf16[1,12,1,1024]{3,2,1,0:T(2,128)(2,1)S(1)}, u32[]{:S(2)}) copy-start(bf16[1,12,1,1024]{3,2,1,0:T(2,128)(2,1)S(1)} %get-tuple-element.38) | copy-start | bytes 73732
  38.1 2.9 %copy-start.44 = (bf16[1,12,1,1024]{3,2,1,0:T(2,128)(2,1)}, bf16[1,12,1,1024]{3,2,1,0:T(2,128)(2,1)S(1)}, u32[]{:S(2)}) copy-start(bf16[1,12,1,1024]{3,2,1,0:T(2,128)(2,1)S(1)} %get-tuple-element.24) | copy-start | bytes 73732
  41.0 4.2 %copy-start.67 = (f32[1,256]{1,0:T(1,128)S(1)}, f32[1,256]{1,0:T(1,128)}, u32[]{:S(2)}) copy-start(f32[1,256]{1,0:T(1,128)} %param.16) | copy-start | bytes 3076
  41.3 8.9 %copy-start.69 = (f32[1,256]{1,0:T(1,128)S(1)}, f32[1,256]{1,0:T(1,128)}, u32[]{:S(2)}) copy-start(f32[1,256]{1,0:T(1,128)} %param.15) | copy-start | bytes 3076
  41.3 9.9 %copy-start.3 = (f32[1,5,12,1024]{3,0,2,1:T(1,128)S(1)}, f32[1,5,12,1024]{3,0,2,1:T(1,128)}, u32[]{:S(2)}) copy-start(f32[1,5,12,1024]{3,0,2,1:T(1,128)} %param.10) | copy-start | bytes 737284
  42.2 12.7 %copy-start.50 = (bf16[1,12,1,1024]{3,2,1,0:T(2,128)(2,1)S(1)}, bf16[1,12,1,1024]{3,2,1,0:T(2,128)(2,1)}, u32[]{:S(2)}) copy-start(bf16[1,12,1,1024]{3,2,1,0:T(2,128)(2,1)} %get-tuple-element.60) | copy-start | bytes 73732
  42.2 12.7 %copy-start.54 = (bf16[1,12,1,1024]{3,2,1,0:T(2,128)(2,1)S(1)}, bf16[1,12,1,1024]{3,2,1,0:T(2,128)(2,1)}, u32[]{:S(2)}) copy-start(bf16[1,12,1,1024]{3,2,1,0:T(2,128)(2,1)} %get-tuple-element.61) | copy-start | bytes 73732
  42.4 13.3 %copy-start.49 = (bf16[1,12,1,1024]{3,2,1,0:T(2,128)(2,1)S(1)}, bf16[1,12,1,1024]{3,2,1,0:T(2,128)(2,1)}, u32[]{:S(2)}) copy-start(bf16[1,12,1,1024]{3,2,1,0:T(2,128)(2,1)} %get-tuple-element.55) | copy-start | bytes 73732
  42.4 13.4 %copy-start.53 = (bf16[1,12,1,1024]{3,2,1,0:T(2,128)(2,1)S(1)}, bf16[1,12,1,1024]{3,2,1,0:T(2,128)(2,1)}, u32[]{:S(2)}) copy-start(bf16[1,12,1,1024]{3,2,1,0:T(2,128)(2,1)} %get-tuple-element.56) | copy-start | bytes 73732
  42.4 13.4 %copy-start.60 = (bf16[1,12,1,1024]{3,2,1,0:T(2,128)(2,1)S(1)}, bf16[1,12,1,1024]{3,2,1,0:T(2,128)(2,1)}, u32[]{:S(2)}) copy-start(bf16[1,12,1,1024]{3,2,1,0:T(2,128)(2,1)} %get-tuple-element.57) | copy-start | bytes 73732
  42.7 14.0 %copy-start.56 = (bf16[1,12,1,1024]{3,2,1,0:T(2,128)(2,1)S(1)}, bf16[1,12,1,1024]{3,2,1,0:T(2,128)(2,1)}, u32[]{:S(2)}) copy-start(bf16[1,12,1,1024]{3,2,1,0:T(2,128)(2,1)} %get-tuple-element.48) | copy-start | bytes 73732
  43.1 14.5 %copy-start.48 = (bf16[1,12,1,1024]{3,2,1,0:T(2,128)(2,1)S(1)}, bf16[1,12,1,1024]{3,2,1,0:T(2,128)(2,1)}, u32[]{:S(2)}) copy-start(bf16[1,12,1,1024]{3,2,1,0:T(2,128)(2,1)} %get-tuple-element.50) | copy-start | bytes 73732
  43.1 14.5 %copy-start.52 = (bf16[1,12,1,1024]{3,2,1,0:T(2,128)(2,1)S(1)}, bf16[1,12,1,1024]{3,2,1,0:T(2,128)(2,1)}, u32[]{:S(2)}) copy-start(bf16[1,12,1,1024]{3,2,1,0:T(2,128)(2,1)} %get-tuple-element.51) | copy-start | bytes 73732
  43.1 14.5 %copy-start.59 = (bf16[1,12,1,1024]{3,2,1,0:T(2,128)(2,1)S(1)}, bf16[1,12,1,1024]{3,2,1,0:T(2,128)(2,1)}, u32[]{:S(2)}) copy-start(bf16[1,12,1,1024]{3,2,1,0:T(2,128)(2,1)} %get-tuple-element.52) | copy-start | bytes 73732
  46.1 32.8 %collective-permute-start.3 = (f32[1,5,12,256]{3,2,1,0:T(8,128)}, f32[1,5,12,256]{3,2,1,0:T(8,128)}, u32[]{:S(2)}, u32[]{:S(2)}) collective-permute-start(f32[1,5,12,256]{3,2,1,0:T(8,128)} %fusion.11), channel_id=1, source_target_pairs={{2,0},{4,2},{6,4},{8,6},{10,8},{12,10},{14,12},{16,14},{18,16},{20... | collective-permute-start | bytes 184328 | tf_op jit(solution)/shard_map/ppermute | solution.py:16
  48.1 10.4 %copy-start.55 = (bf16[1,12,1,1024]{3,2,1,0:T(2,128)(2,1)S(1)}, bf16[1,12,1,1024]{3,2,1,0:T(2,128)(2,1)}, u32[]{:S(2)}) copy-start(bf16[1,12,1,1024]{3,2,1,0:T(2,128)(2,1)} %get-tuple-element.47) | copy-start | bytes 73732
  51.2 8.2 %copy-start.47 = (bf16[1,12,1,1024]{3,2,1,0:T(2,128)(2,1)S(1)}, bf16[1,12,1,1024]{3,2,1,0:T(2,128)(2,1)}, u32[]{:S(2)}) copy-start(bf16[1,12,1,1024]{3,2,1,0:T(2,128)(2,1)} %get-tuple-element.45) | copy-start | bytes 73732
  51.2 8.2 %copy-start.51 = (bf16[1,12,1,1024]{3,2,1,0:T(2,128)(2,1)S(1)}, bf16[1,12,1,1024]{3,2,1,0:T(2,128)(2,1)}, u32[]{:S(2)}) copy-start(bf16[1,12,1,1024]{3,2,1,0:T(2,128)(2,1)} %get-tuple-element.46) | copy-start | bytes 73732
  51.2 8.2 %copy-start.58 = (bf16[1,12,1,1024]{3,2,1,0:T(2,128)(2,1)S(1)}, bf16[1,12,1,1024]{3,2,1,0:T(2,128)(2,1)}, u32[]{:S(2)}) copy-start(bf16[1,12,1,1024]{3,2,1,0:T(2,128)(2,1)} %copy-done.57) | copy-start | bytes 73732
  51.2 32.7 %collective-permute-start.2 = (f32[1,5,12,256]{3,2,1,0:T(8,128)}, f32[1,5,12,256]{3,2,1,0:T(8,128)}, u32[]{:S(2)}, u32[]{:S(2)}) collective-permute-start(f32[1,5,12,256]{3,2,1,0:T(8,128)} %fusion.9), channel_id=1, source_target_pairs={{30,0},{0,2},{2,4},{4,6},{6,8},{8,10},{10,12},{12,14},{14,16},{16,... | collective-permute-start | bytes 184328 | tf_op jit(solution)/shard_map/ppermute | solution.py:16
  57.6 5.4 %copy-start.66 = (f32[1,1024]{1,0:T(1,128)S(1)}, f32[1,1024]{1,0:T(1,128)}, u32[]{:S(2)}) copy-start(f32[1,1024]{1,0:T(1,128)} %param.14) | copy-start | bytes 12292
  58.6 5.6 %copy-start.68 = (f32[1,256]{1,0:T(1,128)S(1)}, f32[1,256]{1,0:T(1,128)}, u32[]{:S(2)}) copy-start(f32[1,256]{1,0:T(1,128)} %param.16) | copy-start | bytes 3076
  60.3 4.8 %copy-start.4 = (f32[1,5,12,1024]{3,2,1,0:T(8,128)}, f32[1,5,12,1024]{3,2,1,0:T(8,128)S(1)}, u32[]{:S(2)}) copy-start(f32[1,5,12,1024]{3,2,1,0:T(8,128)S(1)} %get-tuple-element.78) | copy-start | bytes 737284
  74.4 3.0 %copy-start.9 = (bf16[1,12,1,1024]{3,2,1,0:T(2,128)(2,1)S(1)}, bf16[1,12,1,1024]{3,2,1,0:T(2,128)(2,1)}, u32[]{:S(2)}) copy-start(bf16[1,12,1,1024]{3,2,1,0:T(2,128)(2,1)} %copy-done.8) | copy-start | bytes 73732
  74.4 3.1 %copy-start.37 = (bf16[1,12,1,1024]{3,2,1,0:T(2,128)(2,1)S(1)}, bf16[1,12,1,1024]{3,2,1,0:T(2,128)(2,1)}, u32[]{:S(2)}) copy-start(bf16[1,12,1,1024]{3,2,1,0:T(2,128)(2,1)} %copy-done.36) | copy-start | bytes 73732
  74.4 3.1 %copy-start.39 = (bf16[1,12,1,1024]{3,2,1,0:T(2,128)(2,1)S(1)}, bf16[1,12,1,1024]{3,2,1,0:T(2,128)(2,1)}, u32[]{:S(2)}) copy-start(bf16[1,12,1,1024]{3,2,1,0:T(2,128)(2,1)} %copy-done.38) | copy-start | bytes 73732
  74.4 3.1 %copy-start.41 = (bf16[1,12,1,1024]{3,2,1,0:T(2,128)(2,1)S(1)}, bf16[1,12,1,1024]{3,2,1,0:T(2,128)(2,1)}, u32[]{:S(2)}) copy-start(bf16[1,12,1,1024]{3,2,1,0:T(2,128)(2,1)} %copy-done.40) | copy-start | bytes 73732
  74.4 3.1 %copy-start.43 = (bf16[1,12,1,1024]{3,2,1,0:T(2,128)(2,1)S(1)}, bf16[1,12,1,1024]{3,2,1,0:T(2,128)(2,1)}, u32[]{:S(2)}) copy-start(bf16[1,12,1,1024]{3,2,1,0:T(2,128)(2,1)} %copy-done.42) | copy-start | bytes 73732
  74.4 3.1 %copy-start.7 = (bf16[1,12,1,1024]{3,2,1,0:T(2,128)(2,1)S(1)}, bf16[1,12,1,1024]{3,2,1,0:T(2,128)(2,1)}, u32[]{:S(2)}) copy-start(bf16[1,12,1,1024]{3,2,1,0:T(2,128)(2,1)} %copy-done.6) | copy-start | bytes 73732
  74.4 3.1 %copy-start.29 = (bf16[1,12,1,1024]{3,2,1,0:T(2,128)(2,1)S(1)}, bf16[1,12,1,1024]{3,2,1,0:T(2,128)(2,1)}, u32[]{:S(2)}) copy-start(bf16[1,12,1,1024]{3,2,1,0:T(2,128)(2,1)} %copy-done.28) | copy-start | bytes 73732
  74.4 3.1 %copy-start.31 = (bf16[1,12,1,1024]{3,2,1,0:T(2,128)(2,1)S(1)}, bf16[1,12,1,1024]{3,2,1,0:T(2,128)(2,1)}, u32[]{:S(2)}) copy-start(bf16[1,12,1,1024]{3,2,1,0:T(2,128)(2,1)} %copy-done.30) | copy-start | bytes 73732
  74.4 3.1 %copy-start.33 = (bf16[1,12,1,1024]{3,2,1,0:T(2,128)(2,1)S(1)}, bf16[1,12,1,1024]{3,2,1,0:T(2,128)(2,1)}, u32[]{:S(2)}) copy-start(bf16[1,12,1,1024]{3,2,1,0:T(2,128)(2,1)} %copy-done.32) | copy-start | bytes 73732
  74.4 3.1 %copy-start.35 = (bf16[1,12,1,1024]{3,2,1,0:T(2,128)(2,1)S(1)}, bf16[1,12,1,1024]{3,2,1,0:T(2,128)(2,1)}, u32[]{:S(2)}) copy-start(bf16[1,12,1,1024]{3,2,1,0:T(2,128)(2,1)} %copy-done.34) | copy-start | bytes 73732
  74.4 3.2 %copy-start.21 = (bf16[1,12,1,1024]{3,2,1,0:T(2,128)(2,1)S(1)}, bf16[1,12,1,1024]{3,2,1,0:T(2,128)(2,1)}, u32[]{:S(2)}) copy-start(bf16[1,12,1,1024]{3,2,1,0:T(2,128)(2,1)} %copy-done.20) | copy-start | bytes 73732
  74.5 3.2 %copy-start.23 = (bf16[1,12,1,1024]{3,2,1,0:T(2,128)(2,1)S(1)}, bf16[1,12,1,1024]{3,2,1,0:T(2,128)(2,1)}, u32[]{:S(2)}) copy-start(bf16[1,12,1,1024]{3,2,1,0:T(2,128)(2,1)} %copy-done.22) | copy-start | bytes 73732
  74.5 3.2 %copy-start.25 = (bf16[1,12,1,1024]{3,2,1,0:T(2,128)(2,1)S(1)}, bf16[1,12,1,1024]{3,2,1,0:T(2,128)(2,1)}, u32[]{:S(2)}) copy-start(bf16[1,12,1,1024]{3,2,1,0:T(2,128)(2,1)} %copy-done.24) | copy-start | bytes 73732
  74.5 3.2 %copy-start.27 = (bf16[1,12,1,1024]{3,2,1,0:T(2,128)(2,1)S(1)}, bf16[1,12,1,1024]{3,2,1,0:T(2,128)(2,1)}, u32[]{:S(2)}) copy-start(bf16[1,12,1,1024]{3,2,1,0:T(2,128)(2,1)} %copy-done.26) | copy-start | bytes 73732
  74.5 3.3 %copy-start.13 = (bf16[1,12,1,1024]{3,2,1,0:T(2,128)(2,1)S(1)}, bf16[1,12,1,1024]{3,2,1,0:T(2,128)(2,1)}, u32[]{:S(2)}) copy-start(bf16[1,12,1,1024]{3,2,1,0:T(2,128)(2,1)} %copy-done.12) | copy-start | bytes 73732
  74.5 3.3 %copy-start.15 = (bf16[1,12,1,1024]{3,2,1,0:T(2,128)(2,1)S(1)}, bf16[1,12,1,1024]{3,2,1,0:T(2,128)(2,1)}, u32[]{:S(2)}) copy-start(bf16[1,12,1,1024]{3,2,1,0:T(2,128)(2,1)} %copy-done.14) | copy-start | bytes 73732
  74.5 3.3 %copy-start.17 = (bf16[1,12,1,1024]{3,2,1,0:T(2,128)(2,1)S(1)}, bf16[1,12,1,1024]{3,2,1,0:T(2,128)(2,1)}, u32[]{:S(2)}) copy-start(bf16[1,12,1,1024]{3,2,1,0:T(2,128)(2,1)} %copy-done.16) | copy-start | bytes 73732
  74.5 3.3 %copy-start.19 = (bf16[1,12,1,1024]{3,2,1,0:T(2,128)(2,1)S(1)}, bf16[1,12,1,1024]{3,2,1,0:T(2,128)(2,1)}, u32[]{:S(2)}) copy-start(bf16[1,12,1,1024]{3,2,1,0:T(2,128)(2,1)} %copy-done.18) | copy-start | bytes 73732
  85.9 3.1 %copy-start = (f32[1,5,24,1024]{3,0,1,2:T(1,128)S(1)}, f32[1,5,24,1024]{3,0,1,2:T(1,128)}, u32[]{:S(2)}) copy-start(f32[1,5,24,1024]{3,0,1,2:T(1,128)} %all_gather.21) | copy-start | bytes 1474564
  85.9 3.1 %copy-start.2 = (f32[1,5,12,1023]{3,2,1,0:T(8,128)S(1)}, f32[1,5,12,1023]{3,2,1,0:T(8,128)}, u32[]{:S(2)}) copy-start(f32[1,5,12,1023]{3,2,1,0:T(8,128)} %slice_multiply_fusion) | copy-start | bytes 736564
  85.9 3.1 %copy-start.65 = (f32[24,24]{1,0:T(8,128)S(1)}, f32[24,24]{1,0:T(8,128)}, u32[]{:S(2)}) copy-start(f32[24,24]{1,0:T(8,128)} %get-tuple-element.86) | copy-start | bytes 6916
  (11 other events, 26.3 us)
where the time goes:
time: 93 us; the launch traced here: 91.7 us
  local copies, waits for them, and re-layouts  39.6 us (43%)
  other arithmetic  21.2 us (23%)
  blocking collectives  12.8 us (14%)
  starting transfers between devices  8.88 us (10%)
  matrix products  7.34 us (8%)
  between operations  1.92 us (2%)
    broadcast_in_dim x8, local copies, waits for them, and re-layouts, face_spread(): return jnp.repeat(values, 4, axis=-1) * mask  12.2 us
    ppermute x4, starting transfers between devices, passed_along(): return lax.ppermute(block, axis, route)  8.88 us
    unnamed x13, other arithmetic  8.42 us
    dot_general x6, matrix products, instance_mix(): jnp.einsum('ts,pvsc->pvtc', matrix, vector, precision=lax.Precision.HIGHEST)  7.34 us
    reduce_sum x3, other arithmetic, face_pick(): return jnp.sum(picked, axis=-1)  6.04 us
    slice x2, local copies, waits for them, and re-layouts, block_apply(): blocks[:, :, row_index * variables + column_index, :]  5.68 us
    all_gather x2, blocking collectives, regroup(): lax.all_gather(vector, 'inst', axis=2, tiled=True)  4.67 us
    all_gather x2, blocking collectives, regroup(): lax.all_gather(up_face, 'inst', axis=2, tiled=True)  4.12 us
  transfers between devices with their start and end apart: 4, of which 0 were waited for; matrix products, arithmetic and copies ran while one was open for 51% of the time, Pallas kernels for 0%

commit v1 on v0

v1 whole, which is shorter than its diff:
```python
import functools
import math

import jax
import jax.numpy as jnp
import numpy as np
from jax import lax
from jax.experimental import pallas as pl
from jax.experimental.pallas import tpu as pltpu
from jax.sharding import PartitionSpec as P

OMEGA = 0.15
NV = 5
NH = 11
NT = 24
OWN = 12
ROWS = 16
VR = NV * ROWS
FR = 64
MESH = pl.DeviceIdType.MESH
F32 = jnp.float32
BF16 = jnp.bfloat16


def constants():
    t = np.arange(NT)
    d = t[:, None] - t[None, :]
    skewed = np.zeros((NT, NT))
    for k in range(1, NH + 1):
        skewed -= 2.0 / NT * k * np.sin(2 * np.pi * ((k * d) % NT) / NT)
    derivative = 0.5 * skewed - 0.5 * skewed.T
    big = np.zeros((NV, ROWS, 2, NV, ROWS))
    for j in range(NV):
        for h in range(2):
            big[j, :OWN, h, j, :OWN] = OMEGA * derivative[:OWN, h * OWN : (h + 1) * OWN]
    big = big.reshape(VR, 2 * VR).astype(np.float32)
    hi = big.astype(BF16)
    lo = (big - hi.astype(np.float32)).astype(BF16)
    deriv = np.concatenate([hi, lo], 0)
    a1 = np.zeros((FR, 128))
    a2 = np.zeros((FR, 128))
    f = np.zeros((128, 2, NV, ROWS))
    order = np.full((1, 128), -1, np.int32)
    tt = np.arange(OWN)
    for j in range(NV):
        rows = j * OWN + tt
        for m in range(NT):
            lane = j * NT + m
            k = (m + 1) // 2
            for h in range(2):
                s = tt + h * OWN
                if m == 0:
                    f[lane, h, j, :OWN] = 1.0 / NT
                elif m == NT - 1:
                    f[lane, h, j, :OWN] = (1.0 - 2.0 * (s % 2)) / NT
                elif m % 2 == 1:
                    f[lane, h, j, :OWN] = 2.0 / NT * np.cos(2 * np.pi * ((k * s) % NT) / NT)
                else:
                    f[lane, h, j, :OWN] = 2.0 / NT * np.sin(2 * np.pi * ((k * s) % NT) / NT)
            arc = 2 * np.pi * ((k * tt) % NT) / NT
            if m == 0:
                a1[rows, lane] = 1.0
            elif m == NT - 1:
                a1[rows, lane] = 1.0 - 2.0 * (tt % 2)
            elif m % 2 == 1:
                a1[rows, lane], a2[rows, lane] = np.cos(arc), np.sin(arc)
                order[0, lane] = k - 1
            else:
                a1[rows, lane], a2[rows, lane] = np.sin(arc), -np.cos(arc)
                order[0, lane] = k - 1
    f = f.reshape(128, 2 * VR)
    perm = np.zeros((NV * NV, ROWS, OWN, 32), np.float32)
    for e in range(NV * NV):
        for i in range(OWN):
            perm[e, i, i, e] = 1.0
    perm = perm.reshape(NV * NV * ROWS, OWN * 32).astype(BF16)
    return (
        deriv,
        np.concatenate([a1, a2], 0).astype(np.float32),
        f.astype(np.float32),
        order,
        perm,
    )


def split(x):
    hi = x.astype(BF16)
    return hi, (x - hi.astype(F32)).astype(BF16)


def dot(a, b):
    return jnp.dot(a, b, preferred_element_type=F32)


def dot_t(a, b):
    return lax.dot_general(a, b, (((1,), (1,)), ((), ())), preferred_element_type=F32)


def kernel(
    passages,
    tan_hbm, adj_hbm, jac_hbm, pre_hbm, upwind_ref, upw_ref, bot_ref, up_ref, lo_ref, phase_ref,
    deriv_ref, a_ref, f_ref, order_ref, perm_ref,
    tan_out, adj_out,
    tan_own, adj_own, tan_far, jac, pre, mpad, jt, pt,
    vt, vd, vfar, dual_far, sel_lo, sel_up, send, recv, spread, img, stage, adj_stage,
    in_sem, out_sem, send_sem, recv_sem,
):
    blade, inst = lax.axis_index("blade"), lax.axis_index("inst")
    ring = lax.axis_size("blade")
    nxt = {"blade": lax.rem(blade + 1, ring)}
    prv = {"blade": lax.rem(blade + ring - 1, ring)}
    sib = {"inst": 1 - inst}

    loads = [
        pltpu.make_async_copy(src.at[0], dst, in_sem.at[n])
        for n, (src, dst) in enumerate(
            ((adj_hbm, adj_own), (pre_hbm, pre), (tan_hbm, tan_own), (jac_hbm, jac))
        )
    ]
    for copy in loads:
        copy.start()

    barrier = pltpu.get_barrier_semaphore()
    for device in (sib, prv, nxt):
        pl.semaphore_signal(barrier, inc=1, device_id=device, device_id_type=MESH)

    def remote(n, src, dst, device):
        return pltpu.make_async_remote_copy(
            src_ref=src, dst_ref=dst, send_sem=send_sem.at[n], recv_sem=recv_sem.at[n],
            device_id=device, device_id_type=MESH,
        )

    send_tan = remote(0, tan_hbm.at[0], tan_far, sib)
    send_dual = remote(1, vd, dual_far, sib)
    face_sends = [
        remote(2, send.at[0], recv.at[0], prv),
        remote(3, send.at[1], recv.at[1], nxt),
        remote(4, send.at[2], recv.at[2], prv),
        remote(5, send.at[3], recv.at[3], nxt),
    ]

    pl.semaphore_wait(barrier, 3)
    send_tan.start()

    order = order_ref[...]
    index = jnp.zeros((1, 128), F32)
    for k in range(NH):
        index = jnp.where(order == k, phase_ref[k].astype(F32), index)
    angle = (2.0 * math.pi / passages) * index
    cosine, sine = jnp.cos(angle), jnp.sin(angle)
    a1, a2 = a_ref[:FR], a_ref[FR:]
    both = jnp.concatenate([a1 * cosine + a2 * sine, a1 * cosine - a2 * sine], 0)
    rot = jnp.dot(both, f_ref[...], preferred_element_type=F32, precision=lax.Precision.HIGHEST)
    rot_lo, rot_up = [jnp.concatenate(split(rot[n * FR : (n + 1) * FR]), 0) for n in range(2)]

    for table, sel in ((lo_ref, sel_lo), (up_ref, sel_up)):
        for h in range(2):
            cells = lax.broadcasted_iota(jnp.int32, (512, 128), 0) + 512 * h
            hit = cells == table[:, 128 * h : 128 * h + 128]
            sel[h] = jnp.where(hit, 1.0, 0.0).astype(BF16)

    vt[...] = jnp.zeros_like(vt)
    vfar[...] = jnp.zeros_like(vfar)
    mpad[...] = jnp.zeros_like(mpad)
    spread[...] = jnp.zeros_like(spread)

    def regroup(src, dst):
        for t in range(OWN):
            mpad[t, 0:25, :] = src[t]
        for n in range(4):
            lanes = slice(256 * n, 256 * n + 256)
            part = mpad[:, :, lanes].reshape(OWN * 32, 256)
            dst[:, :, lanes] = dot(perm_ref[...], part).reshape(NV * NV, ROWS, 256)

    def block(m, src, i, lanes, transposed):
        total = None
        for j in range(NV):
            e = j * NV + i if transposed else i * NV + j
            term = m[e, :, lanes] * src[j, :, lanes]
            total = term if total is None else total + term
        return total

    loads[0].wait()
    loads[1].wait()
    for j in range(NV):
        vfar[j, 0:OWN, :] = adj_own[j]
    regroup(pre, pt)
    for n in range(8):
        lanes = slice(128 * n, 128 * n + 128)
        for i in range(NV):
            vd[i, :, lanes] = block(pt, vfar, i, lanes, True)
    send_dual.start()

    def faces(field_hi, field_lo, base):
        halves = jnp.concatenate([field_hi, field_lo], 0)
        for n, (sel, rotation) in enumerate(((sel_lo, rot_lo), (sel_up, rot_up))):
            picked = jnp.concatenate(
                [dot(halves[:, 512 * h : 512 * h + 512], sel[h]) for h in range(2)], 1
            ).astype(BF16)
            turned = dot(rotation, picked[: 2 * VR])
            total = turned[:FR] + turned[FR:] + dot(rotation[:FR], picked[2 * VR :])
            if base == 2:
                total = total * (bot_ref[...] if n == 0 else upw_ref[...])
            send[base + n] = total
            face_sends[base + n].start()

    def mixed(field_hi, field_lo):
        twice = dot(deriv_ref[...], field_hi)
        return twice[:VR] + twice[VR:] + dot(deriv_ref[:VR], field_lo)

    def field(own, far):
        return split(jnp.concatenate([own.reshape(VR, 1024), far.reshape(VR, 1024)], 0))

    loads[2].wait()
    for j in range(NV):
        vt[j, 0:OWN, :] = tan_own[j]
    send_tan.wait()
    for j in range(NV):
        vfar[j, 0:OWN, :] = tan_far[j]
    tan_hi, tan_lo = field(vt[...], vfar[...])
    faces(tan_hi, tan_lo, 0)
    img[0] = mixed(tan_hi, tan_lo).reshape(NV, ROWS, 1024)

    send_dual.wait()
    dual_hi, dual_lo = field(vd[...], dual_far[...])
    faces(dual_hi, dual_lo, 2)
    img[1] = -mixed(dual_hi, dual_lo).reshape(NV, ROWS, 1024)

    loads[3].wait()
    regroup(jac, jt)
    lane = lax.broadcasted_iota(jnp.int32, (ROWS, 1024), 1)
    upwind = upwind_ref[...]
    for i in range(NV):
        before = jnp.where(lane == 0, 0.0, pltpu.roll(vt[i], 1, 1))
        img[0, i] = img[0, i] - upwind * before
        after = jnp.where(lane == 1023, 0.0, pltpu.roll(upwind * vd[i], 1023, 1))
        img[1, i] = img[1, i] - after
    for n in range(8):
        lanes = slice(128 * n, 128 * n + 128)
        for i in range(NV):
            img[0, i, :, lanes] = img[0, i, :, lanes] + block(jt, vt, i, lanes, False)
            img[1, i, :, lanes] = img[1, i, :, lanes] + block(jt, vd, i, lanes, True)

    def add_faces(base, scales):
        for n in range(2):
            for j in range(NV):
                got = recv[base + n, j * OWN : j * OWN + OWN, :]
                spread[n, j, 0:OWN, :] = got if scales is None else got * scales[n][...]
        pair = [jnp.concatenate(split(spread[n].reshape(VR, 256)), 0) for n in range(2)]
        for h in range(2):
            cells = slice(512 * h, 512 * h + 512)
            part = slice(128 * h, 128 * h + 128)
            total = dot_t(pair[0][:, part], sel_up[h]) + dot_t(pair[1][:, part], sel_lo[h])
            total = (total[:VR] + total[VR:]).reshape(NV, ROWS, 512)
            img[base // 2, :, :, cells] = img[base // 2, :, :, cells] - total

    for copy in face_sends[:2]:
        copy.wait()
    add_faces(0, (upw_ref, bot_ref))
    for n in range(8):
        lanes = slice(128 * n, 128 * n + 128)
        for i in range(NV):
            stage[i, :, lanes] = block(pt, img.at[0], i, lanes, False)[:OWN]
    tan_store = pltpu.make_async_copy(stage, tan_out.at[0], out_sem.at[0])
    tan_store.start()

    for copy in face_sends[2:]:
        copy.wait()
    add_faces(2, None)
    adj_stage[...] = img[1, :, 0:OWN, :]
    adj_store = pltpu.make_async_copy(adj_stage, adj_out.at[0], out_sem.at[1])
    adj_store.start()
    tan_store.wait()
    adj_store.wait()


def on_device(
    tangent_seed, adjoint_seed, jacobian, precond, upwind, up_weight, bottom_face_strength,
    up_cells, lo_cells, phase_index,
):
    passages = tangent_seed.shape[0] * lax.axis_size("blade")
    deriv, a, f, order, perm = constants()
    field = (NV, ROWS, 1024)
    whole = pl.BlockSpec(memory_space=pltpu.VMEM)
    hbm = pl.BlockSpec(memory_space=pl.ANY)
    return pl.pallas_call(
        functools.partial(kernel, passages),
        out_shape=(
            jax.ShapeDtypeStruct(tangent_seed.shape, F32),
            jax.ShapeDtypeStruct(adjoint_seed.shape, F32),
        ),
        in_specs=[hbm] * 4 + [whole] * 5 + [pl.BlockSpec(memory_space=pltpu.SMEM)] + [whole] * 5,
        out_specs=(hbm, hbm),
        scratch_shapes=[
            pltpu.VMEM((NV, OWN, 1024), F32),
            pltpu.VMEM((NV, OWN, 1024), F32),
            pltpu.VMEM((NV, OWN, 1024), F32),
            pltpu.VMEM((OWN, 25, 1024), BF16),
            pltpu.VMEM((OWN, 25, 1024), BF16),
            pltpu.VMEM((OWN, 32, 1024), BF16),
            pltpu.VMEM((25, ROWS, 1024), F32),
            pltpu.VMEM((25, ROWS, 1024), F32),
            pltpu.VMEM(field, F32),
            pltpu.VMEM(field, F32),
            pltpu.VMEM(field, F32),
            pltpu.VMEM(field, F32),
            pltpu.VMEM((2, 512, 128), BF16),
            pltpu.VMEM((2, 512, 128), BF16),
            pltpu.VMEM((4, FR, 256), F32),
            pltpu.VMEM((4, FR, 256), F32),
            pltpu.VMEM((2, NV, ROWS, 256), F32),
            pltpu.VMEM((2,) + field, F32),
            pltpu.VMEM((NV, OWN, 1024), F32),
            pltpu.VMEM((NV, OWN, 1024), F32),
            pltpu.SemaphoreType.DMA((4,)),
            pltpu.SemaphoreType.DMA((2,)),
            pltpu.SemaphoreType.DMA((6,)),
            pltpu.SemaphoreType.DMA((6,)),
        ],
        compiler_params=pltpu.CompilerParams(
            collective_id=0, has_side_effects=True, vmem_limit_bytes=48 * 1024 * 1024
        ),
        name="harmonic_blade_row",
    )(
        tangent_seed, adjoint_seed, jacobian, precond, upwind, up_weight, bottom_face_strength,
        up_cells.reshape(1, -1), lo_cells.reshape(1, -1), phase_index,
        deriv, a, f, order, perm,
    )


def solution(mesh):
    in_specs = (
        P("blade", None, "inst", None),
        P("blade", None, "inst", None),
        P("blade", "inst", None, None),
        P("blade", "inst", None, None),
        P("blade", None),
        P("blade", None),
        P("blade", None),
        P(),
        P(),
        P(),
    )
    out_specs = (P("blade", None, "inst", None), P("blade", None, "inst", None))
    return jax.shard_map(
        on_device, mesh=mesh, in_specs=in_specs, out_specs=out_specs, check_vma=False
    )
```

time: 93 us -> 24.5 us (0.26)
  local copies, waits for them, and re-layouts: 39.6 us -> 7.88 us
  other arithmetic: 21.2 us -> 0 us
  Pallas kernels: 0 us -> 15.5 us
  blocking collectives: 12.8 us -> 0 us
  starting transfers between devices: 8.88 us -> 0 us
  matrix products: 7.34 us -> 0 us
  between operations: 1.92 us -> 0.8 us
    pallas_call x0 -> x1, Pallas kernels: none -> 15.5 us  [on_device(): pl.pallas_call(functools.partial(kernel, passages), out_shape=(jax.ShapeD...]
    all_gather x6 -> x0, blocking collectives: 12.8 us -> none  [the longest x2 4.67 us: regroup(): lax.all_gather(vector, 'inst', axis=2, tiled=True)]
    broadcast_in_dim x10 -> x0, local copies, waits for them, and re-layouts: 12.4 us -> none  [the longest x8 12.2 us: face_spread(): return jnp.repeat(values, 4, axis=-1) * mask]
    ppermute x4 -> x0, starting transfers between devices: 8.88 us -> none  [passed_along(): return lax.ppermute(block, axis, route)]
    unnamed x13 -> x0, other arithmetic: 8.42 us -> none
    slice x6 -> x0, local copies, waits for them, and re-layouts: 8.1 us -> none  [the longest x2 5.68 us: block_apply(): blocks[:, :, row_index * variables + column_index, :]]
    reduce_sum x4 -> x0, other arithmetic: 7.69 us -> none  [the longest x3 6.04 us: face_pick(): return jnp.sum(picked, axis=-1)]
    dot_general x6 -> x0, matrix products: 7.34 us -> none  [instance_mix(): jnp.einsum('ts,pvsc->pvtc', matrix, vector, precision=lax.Precision.HIGHEST)]
  transfers between devices with their start and end apart: 4 -> 0, of which waited for: 0 -> 0; matrix products, arithmetic and copies ran while one was open for 51% -> 0% of each run, Pallas kernels for 0% -> 0%
where the time goes in v1:
time: 24.5 us; the launch traced here: 24.2 us
  Pallas kernels  15.5 us (63%)
  local copies, waits for them, and re-layouts  7.88 us (32%)
  between operations  0.8 us (3%)
    pallas_call x1, Pallas kernels, on_device(): pl.pallas_call(functools.partial(kernel, passages), out_shape=(jax.ShapeD...  15.5 us
    unnamed x28, local copies, waits for them, and re-layouts  5.98 us
    pallas_call x2, local copies, waits for them, and re-layouts, on_device(): pl.pallas_call(functools.partial(kernel, passages), out_shape=(jax.ShapeD...  1.89 us

profile of v1, /device:TPU:0, one launch (start us, length us, event | category | flops | bytes accessed | tf_op | source)
XLA Modules:
  0.0 24.2 jit_solution(17511531222189700115)
XLA Ops:
  0.6 0.0 copy-start
  0.6 1.1 %copy.17.tan_hbm = f32[1,5,12,1024]{3,2,1,0:T(8,128)S(1)} copy(f32[1,5,12,1024]{3,0,2,1:T(1,128)} %param.15) | data formatting | bytes 491520 | tf_op args[0]
  1.7 0.0 copy-start.2
  1.7 0.0 copy-start.6
  1.7 0.0 copy-start.7
  1.7 0.0 copy-start.8
  1.8 0.0 copy-start.9
  1.8 0.0 copy-start.10
  1.8 0.0 copy-start.11
  1.8 0.0 copy-start.12
  1.8 1.1 %copy.18.adj_hbm = f32[1,5,12,1024]{3,2,1,0:T(8,128)S(1)} copy(f32[1,5,12,1024]{3,0,2,1:T(1,128)} %param.16) | data formatting | bytes 491520 | tf_op args[1]
  2.9 0.0 copy-done
  2.9 0.0 copy-done.2
  2.9 0.0 copy-done.6
  2.9 0.0 copy-done.7
  3.0 0.0 copy-done.8
  3.0 0.0 copy-done.9
  3.0 0.0 copy-done.10
  3.0 0.0 copy-done.11
  3.0 0.0 copy-done.12
  3.0 0.0 copy-start.1
  3.0 1.1 %copy-done.1 = bf16[1,12,25,1024]{3,2,1,0:T(8,128)(2,1)S(1)} copy-done((bf16[1,12,25,1024]{3,2,1,0:T(8,128)(2,1)S(1)}, bf16[1,12,25,1024]{3,2,1,0:T(8,128)(2,1)}, u32[]{:S(2)}) %copy-start.1) | copy-done | bytes 614424
  4.1 0.0 copy-start.3
  4.1 0.9 %copy-done.3 = f32[128,160]{1,0:T(8,128)S(1)} copy-done((f32[128,160]{1,0:T(8,128)S(1)}, f32[128,160]{1,0:T(8,128)}, u32[]{:S(2)}) %copy-start.3) | copy-done | bytes 81944
  5.0 0.0 copy-start.4
  5.0 0.9 %copy-done.4 = bf16[160,160]{1,0:T(8,128)(2,1)S(1)} copy-done((bf16[160,160]{1,0:T(8,128)(2,1)S(1)}, bf16[160,160]{1,0:T(8,128)(2,1)}, u32[]{:S(2)}) %copy-start.4) | copy-done | bytes 51224
  5.9 0.0 copy-start.5
  5.9 0.8 %copy-done.5 = f32[128,128]{1,0:T(8,128)S(1)} copy-done((f32[128,128]{1,0:T(8,128)S(1)}, f32[128,128]{1,0:T(8,128)}, u32[]{:S(2)}) %copy-start.5) | copy-done | bytes 65560
  6.8 15.5 %harmonic_blade_row.1 = (f32[1,5,12,1024]{3,2,1,0:T(8,128)S(1)}, f32[1,5,12,1024]{3,2,1,0:T(8,128)S(1)}) custom-call(f32[1,5,12,1024]{3,2,1,0:T(8,128)S(1)} %copy.17.tan_hbm, f32[1,5,12,1024]{3,2,1,0:T(8,128)S(1)} %copy.18.adj_hbm, bf16[1,12,25,1024]{3,2,1,0:T(8,128)(2,1)S(1)} %copy-done, bf16[1,12,25,1024]{3,2,1,0:T(8,128)(2,1)S(1)} %copy-done.1, ...), custom_call_target="tpu_custom_call" | custom-call | tf_op jit(solution)/shard_map/harmonic_blade_row/pallas_call | solution.py:286
  22.3 0.9 %copy.19 = f32[1,5,12,1024]{3,0,2,1:T(1,128)} copy(f32[1,5,12,1024]{3,2,1,0:T(8,128)S(1)} %get-tuple-element.2) | data formatting | bytes 491520 | tf_op jit(solution)/shard_map/harmonic_blade_row/pallas_call | solution.py:286
  23.2 0.9 %copy.20 = f32[1,5,12,1024]{3,0,2,1:T(1,128)} copy(f32[1,5,12,1024]{3,2,1,0:T(8,128)S(1)} %get-tuple-element.3) | data formatting | bytes 491520 | tf_op jit(solution)/shard_map/harmonic_blade_row/pallas_call | solution.py:286
Async XLA Ops:
  0.6 2.3 %copy-start = (bf16[1,12,25,1024]{3,2,1,0:T(8,128)(2,1)S(1)}, bf16[1,12,25,1024]{3,2,1,0:T(8,128)(2,1)}, u32[]{:S(2)}) copy-start(bf16[1,12,25,1024]{3,2,1,0:T(8,128)(2,1)} %jac_hbm.1) | copy-start | bytes 1843204
  1.7 1.2 %copy-start.2 = (bf16[400,384]{1,0:T(8,128)(2,1)S(1)}, bf16[400,384]{1,0:T(8,128)(2,1)}, u32[]{:S(2)}) copy-start(bf16[400,384]{1,0:T(8,128)(2,1)} %constant.14.clone.perm_ref) | copy-start | bytes 921604
  1.7 1.2 %copy-start.6 = (f32[1,1024]{1,0:T(1,128)S(1)}, f32[1,1024]{1,0:T(1,128)}, u32[]{:S(2)}) copy-start(f32[1,1024]{1,0:T(1,128)} %upwind_ref.1) | copy-start | bytes 12292
  1.7 1.2 %copy-start.7 = (f32[1,256]{1,0:T(1,128)S(1)}, f32[1,256]{1,0:T(1,128)}, u32[]{:S(2)}) copy-start(f32[1,256]{1,0:T(1,128)} %upw_ref.1) | copy-start | bytes 3076
  1.7 1.2 %copy-start.8 = (f32[1,256]{1,0:T(1,128)S(1)}, f32[1,256]{1,0:T(1,128)}, u32[]{:S(2)}) copy-start(f32[1,256]{1,0:T(1,128)} %bot_ref.1) | copy-start | bytes 3076
  1.8 1.2 %copy-start.9 = (s32[256]{0:T(256)S(1)}, s32[256]{0:T(256)}, u32[]{:S(2)}) copy-start(s32[256]{0:T(256)} %param.22) | copy-start | bytes 3076
  1.8 1.2 %copy-start.10 = (s32[256]{0:T(256)S(1)}, s32[256]{0:T(256)}, u32[]{:S(2)}) copy-start(s32[256]{0:T(256)} %param.23) | copy-start | bytes 3076
  1.8 1.2 %copy-start.11 = (s32[11]{0:T(128)S(1)}, s32[11]{0:T(128)}, u32[]{:S(2)}) copy-start(s32[11]{0:T(128)} %phase_ref.1) | copy-start | bytes 136
  1.8 1.2 %copy-start.12 = (s32[1,128]{1,0:T(1,128)S(1)}, s32[1,128]{1,0:T(1,128)}, u32[]{:S(2)}) copy-start(s32[1,128]{1,0:T(1,128)} %constant.13.clone.order_ref) | copy-start | bytes 1540
  3.0 1.1 %copy-start.1 = (bf16[1,12,25,1024]{3,2,1,0:T(8,128)(2,1)S(1)}, bf16[1,12,25,1024]{3,2,1,0:T(8,128)(2,1)}, u32[]{:S(2)}) copy-start(bf16[1,12,25,1024]{3,2,1,0:T(8,128)(2,1)} %pre_hbm.1) | copy-start | bytes 1843204
  4.1 0.9 %copy-start.3 = (f32[128,160]{1,0:T(8,128)S(1)}, f32[128,160]{1,0:T(8,128)}, u32[]{:S(2)}) copy-start(f32[128,160]{1,0:T(8,128)} %constant.12.clone.f_ref) | copy-start | bytes 245764
  5.0 0.9 %copy-start.4 = (bf16[160,160]{1,0:T(8,128)(2,1)S(1)}, bf16[160,160]{1,0:T(8,128)(2,1)}, u32[]{:S(2)}) copy-start(bf16[160,160]{1,0:T(8,128)(2,1)} %constant.10.clone.deriv_ref) | copy-start | bytes 153604
  5.9 0.8 %copy-start.5 = (f32[128,128]{1,0:T(8,128)S(1)}, f32[128,128]{1,0:T(8,128)}, u32[]{:S(2)}) copy-start(f32[128,128]{1,0:T(8,128)} %constant.11.clone.a_ref) | copy-start | bytes 196612

commit v2 on v1

--- a/solution.py
+++ b/solution.py
@@ -17,6 +17,7 @@
 ROWS = 16
 VR = NV * ROWS
 FR = 64
+VMEM_LIMIT = 63 * 1024 * 1024
 MESH = pl.DeviceIdType.MESH
 F32 = jnp.float32
 BF16 = jnp.bfloat16
@@ -69,17 +70,11 @@
                 a1[rows, lane], a2[rows, lane] = np.sin(arc), -np.cos(arc)
                 order[0, lane] = k - 1
     f = f.reshape(128, 2 * VR)
-    perm = np.zeros((NV * NV, ROWS, OWN, 32), np.float32)
-    for e in range(NV * NV):
-        for i in range(OWN):
-            perm[e, i, i, e] = 1.0
-    perm = perm.reshape(NV * NV * ROWS, OWN * 32).astype(BF16)
     return (
         deriv,
         np.concatenate([a1, a2], 0).astype(np.float32),
         f.astype(np.float32),
         order,
-        perm,
     )
 
 
@@ -98,12 +93,13 @@
 
 def kernel(
     passages,
-    tan_hbm, adj_hbm, jac_hbm, pre_hbm, upwind_ref, upw_ref, bot_ref, up_ref, lo_ref, phase_ref,
-    deriv_ref, a_ref, f_ref, order_ref, perm_ref,
+    tan_hbm, adj_hbm, jac_hbm, pre_hbm, upwind_hbm, upw_hbm, bot_hbm, up_hbm, lo_hbm, phase_hbm,
+    deriv_hbm, a_hbm, f_hbm, order_hbm,
     tan_out, adj_out,
-    tan_own, adj_own, tan_far, jac, pre, mpad, jt, pt,
-    vt, vd, vfar, dual_far, sel_lo, sel_up, send, recv, spread, img, stage, adj_stage,
-    in_sem, out_sem, send_sem, recv_sem,
+    upwind_ref, upw_ref, bot_ref, up_ref, lo_ref, phase_ref, deriv_ref, a_ref, f_ref, order_ref,
+    tan_own, adj_own, tan_far, jac, pre, mpad, perm, jt, pt,
+    vt, vd, va, vfar, dual_far, sel_lo, sel_up, send, recv, spread, img, tan_stage, adj_stage,
+    in_sem, tan_sem, adj_sem, tan_out_sem, adj_out_sem, far_send, far_recv, send_sem, recv_sem,
 ):
     blade, inst = lax.axis_index("blade"), lax.axis_index("inst")
     ring = lax.axis_size("blade")
@@ -111,18 +107,39 @@
     prv = {"blade": lax.rem(blade + ring - 1, ring)}
     sib = {"inst": 1 - inst}
 
-    loads = [
-        pltpu.make_async_copy(src.at[0], dst, in_sem.at[n])
-        for n, (src, dst) in enumerate(
-            ((adj_hbm, adj_own), (pre_hbm, pre), (tan_hbm, tan_own), (jac_hbm, jac))
-        )
-    ]
-    for copy in loads:
-        copy.start()
-
     barrier = pltpu.get_barrier_semaphore()
     for device in (sib, prv, nxt):
         pl.semaphore_signal(barrier, inc=1, device_id=device, device_id_type=MESH)
+
+    def chunk(n):
+        return slice(128 * n, 128 * n + 128)
+
+    def load(n, src, dst):
+        return pltpu.make_async_copy(src, dst, in_sem.at[n])
+
+    def seed_loads(src, dst, sems):
+        return [
+            pltpu.make_async_copy(src.at[:, :, n, 0, :], dst.at[:, :, chunk(n)], sems.at[n])
+            for n in range(8)
+        ]
+
+    first = [
+        load(n, src, dst)
+        for n, (src, dst) in enumerate(
+            (
+                (phase_hbm, phase_ref), (order_hbm, order_ref), (a_hbm, a_ref), (f_hbm, f_ref),
+                (lo_hbm, lo_ref), (up_hbm, up_ref),
+            )
+        )
+    ]
+    tan_loads = seed_loads(tan_hbm, tan_own, tan_sem)
+    adj_loads = seed_loads(adj_hbm, adj_own, adj_sem)
+    pre_load = load(6, pre_hbm.at[0], pre)
+    weights = [load(7, upw_hbm, upw_ref), load(8, bot_hbm, bot_ref), load(9, upwind_hbm, upwind_ref)]
+    deriv_load = load(10, deriv_hbm, deriv_ref)
+    jac_load = load(11, jac_hbm.at[0], jac)
+    for copy in first + tan_loads + [pre_load] + adj_loads + weights + [deriv_load, jac_load]:
+        copy.start()
 
     def remote(n, src, dst, device):
         return pltpu.make_async_remote_copy(
@@ -130,18 +147,38 @@
             device_id=device, device_id_type=MESH,
         )
 
-    send_tan = remote(0, tan_hbm.at[0], tan_far, sib)
-    send_dual = remote(1, vd, dual_far, sib)
+    tan_sends = [
+        pltpu.make_async_remote_copy(
+            src_ref=tan_hbm.at[:, :, n, 0, :], dst_ref=tan_far.at[:, :, chunk(n)],
+            send_sem=far_send.at[n], recv_sem=far_recv.at[n],
+            device_id=sib, device_id_type=MESH,
+        )
+        for n in range(8)
+    ]
+    send_dual = remote(0, vd, dual_far, sib)
     face_sends = [
-        remote(2, send.at[0], recv.at[0], prv),
-        remote(3, send.at[1], recv.at[1], nxt),
-        remote(4, send.at[2], recv.at[2], prv),
-        remote(5, send.at[3], recv.at[3], nxt),
+        remote(1, send.at[0], recv.at[0], prv),
+        remote(2, send.at[1], recv.at[1], nxt),
+        remote(3, send.at[2], recv.at[2], prv),
+        remote(4, send.at[3], recv.at[3], nxt),
     ]
 
+    row = lax.broadcasted_iota(jnp.int32, (NV * NV * ROWS, 1), 0)
+    source = (row & (ROWS - 1)) * 32 + (row >> 4)
+    column = lax.broadcasted_iota(jnp.int32, (NV * NV * ROWS, OWN * 32), 1)
+    perm[...] = jnp.where(column == source, 1.0, 0.0).astype(BF16)
+    vt[:, 8:, :] = jnp.zeros((NV, 8, 1024), F32)
+    va[:, 8:, :] = jnp.zeros((NV, 8, 1024), F32)
+    vfar[:, 8:, :] = jnp.zeros((NV, 8, 1024), F32)
+    mpad[:, 16:, :] = jnp.zeros((OWN, 16, 1024), BF16)
+    spread[:, :, 8:, :] = jnp.zeros((2, NV, 8, 256), F32)
+
     pl.semaphore_wait(barrier, 3)
-    send_tan.start()
-
+    for copy in tan_sends:
+        copy.start()
+
+    for copy in first:
+        copy.wait()
     order = order_ref[...]
     index = jnp.zeros((1, 128), F32)
     for k in range(NH):
@@ -159,18 +196,13 @@
             hit = cells == table[:, 128 * h : 128 * h + 128]
             sel[h] = jnp.where(hit, 1.0, 0.0).astype(BF16)
 
-    vt[...] = jnp.zeros_like(vt)
-    vfar[...] = jnp.zeros_like(vfar)
-    mpad[...] = jnp.zeros_like(mpad)
-    spread[...] = jnp.zeros_like(spread)
-
     def regroup(src, dst):
         for t in range(OWN):
             mpad[t, 0:25, :] = src[t]
         for n in range(4):
             lanes = slice(256 * n, 256 * n + 256)
             part = mpad[:, :, lanes].reshape(OWN * 32, 256)
-            dst[:, :, lanes] = dot(perm_ref[...], part).reshape(NV * NV, ROWS, 256)
+            dst[:, :, lanes] = dot(perm[...], part).reshape(NV * NV, ROWS, 256)
 
     def block(m, src, i, lanes, transposed):
         total = None
@@ -179,17 +211,6 @@
             term = m[e, :, lanes] * src[j, :, lanes]
             total = term if total is None else total + term
         return total
-
-    loads[0].wait()
-    loads[1].wait()
-    for j in range(NV):
-        vfar[j, 0:OWN, :] = adj_own[j]
-    regroup(pre, pt)
-    for n in range(8):
-        lanes = slice(128 * n, 128 * n + 128)
-        for i in range(NV):
-            vd[i, :, lanes] = block(pt, vfar, i, lanes, True)
-    send_dual.start()
 
     def faces(field_hi, field_lo, base):
         halves = jnp.concatenate([field_hi, field_lo], 0)
@@ -211,35 +232,55 @@
     def field(own, far):
         return split(jnp.concatenate([own.reshape(VR, 1024), far.reshape(VR, 1024)], 0))
 
-    loads[2].wait()
+    for copy in tan_loads:
+        copy.wait()
     for j in range(NV):
         vt[j, 0:OWN, :] = tan_own[j]
-    send_tan.wait()
+    for copy in tan_sends:
+        copy.wait()
     for j in range(NV):
         vfar[j, 0:OWN, :] = tan_far[j]
     tan_hi, tan_lo = field(vt[...], vfar[...])
     faces(tan_hi, tan_lo, 0)
+
+    pre_load.wait()
+    regroup(pre, pt)
+    for copy in adj_loads:
+        copy.wait()
+    for j in range(NV):
+        va[j, 0:OWN, :] = adj_own[j]
+    for n in range(8):
+        for i in range(NV):
+            vd[i, :, chunk(n)] = block(pt, va, i, chunk(n), True)
+    send_dual.start()
+
+    for copy in weights:
+        copy.wait()
+    deriv_load.wait()
     img[0] = mixed(tan_hi, tan_lo).reshape(NV, ROWS, 1024)
+    jac_load.wait()
+    regroup(jac, jt)
+    lane = lax.broadcasted_iota(jnp.int32, (ROWS, 1024), 1)
+    upwind = upwind_ref[...]
 
     send_dual.wait()
     dual_hi, dual_lo = field(vd[...], dual_far[...])
     faces(dual_hi, dual_lo, 2)
-    img[1] = -mixed(dual_hi, dual_lo).reshape(NV, ROWS, 1024)
-
-    loads[3].wait()
-    regroup(jac, jt)
-    lane = lax.broadcasted_iota(jnp.int32, (ROWS, 1024), 1)
-    upwind = upwind_ref[...]
+
     for i in range(NV):
         before = jnp.where(lane == 0, 0.0, pltpu.roll(vt[i], 1, 1))
         img[0, i] = img[0, i] - upwind * before
+    for n in range(8):
+        for i in range(NV):
+            img[0, i, :, chunk(n)] = img[0, i, :, chunk(n)] + block(jt, vt, i, chunk(n), False)
+
+    img[1] = -mixed(dual_hi, dual_lo).reshape(NV, ROWS, 1024)
+    for i in range(NV):
         after = jnp.where(lane == 1023, 0.0, pltpu.roll(upwind * vd[i], 1023, 1))
         img[1, i] = img[1, i] - after
     for n in range(8):
-        lanes = slice(128 * n, 128 * n + 128)
         for i in range(NV):
-            img[0, i, :, lanes] = img[0, i, :, lanes] + block(jt, vt, i, lanes, False)
-            img[1, i, :, lanes] = img[1, i, :, lanes] + block(jt, vd, i, lanes, True)
+            img[1, i, :, chunk(n)] = img[1, i, :, chunk(n)] + block(jt, vd, i, chunk(n), True)
 
     def add_faces(base, scales):
         for n in range(2):
@@ -254,24 +295,31 @@
             total = (total[:VR] + total[VR:]).reshape(NV, ROWS, 512)
             img[base // 2, :, :, cells] = img[base // 2, :, :, cells] - total
 
+    def stores(src, dst, sems):
+        return [
+            pltpu.make_async_copy(src.at[:, :, chunk(n)], dst.at[:, :, n, 0, :], sems.at[n])
+            for n in range(8)
+        ]
+
+    tan_stores = stores(tan_stage, tan_out, tan_out_sem)
+    adj_stores = stores(adj_stage, adj_out, adj_out_sem)
+
     for copy in face_sends[:2]:
         copy.wait()
     add_faces(0, (upw_ref, bot_ref))
     for n in range(8):
-        lanes = slice(128 * n, 128 * n + 128)
         for i in range(NV):
-            stage[i, :, lanes] = block(pt, img.at[0], i, lanes, False)[:OWN]
-    tan_store = pltpu.make_async_copy(stage, tan_out.at[0], out_sem.at[0])
-    tan_store.start()
+            tan_stage[i, :, chunk(n)] = block(pt, img.at[0], i, chunk(n), False)[:OWN]
+        tan_stores[n].start()
 
     for copy in face_sends[2:]:
         copy.wait()
     add_faces(2, None)
-    adj_stage[...] = img[1, :, 0:OWN, :]
-    adj_store = pltpu.make_async_copy(adj_stage, adj_out.at[0], out_sem.at[1])
-    adj_store.start()
-    tan_store.wait()
-    adj_store.wait()
+    for n in range(8):
+        adj_stage[:, :, chunk(n)] = img[1, :, 0:OWN, chunk(n)]
+        adj_stores[n].start()
+    for copy in tan_stores + adj_stores:
+        copy.wait()
 
 
 def on_device(
@@ -279,27 +327,37 @@
     up_cells, lo_cells, phase_index,
 ):
     passages = tangent_seed.shape[0] * lax.axis_size("blade")
-    deriv, a, f, order, perm = constants()
+    deriv, a, f, order = constants()
+    own = (NV, OWN, 1024)
     field = (NV, ROWS, 1024)
-    whole = pl.BlockSpec(memory_space=pltpu.VMEM)
+    linear = (NV, OWN, 8, 1, 128)
     hbm = pl.BlockSpec(memory_space=pl.ANY)
-    return pl.pallas_call(
+    tangent_out, adjoint_out = pl.pallas_call(
         functools.partial(kernel, passages),
-        out_shape=(
-            jax.ShapeDtypeStruct(tangent_seed.shape, F32),
-            jax.ShapeDtypeStruct(adjoint_seed.shape, F32),
-        ),
-        in_specs=[hbm] * 4 + [whole] * 5 + [pl.BlockSpec(memory_space=pltpu.SMEM)] + [whole] * 5,
+        out_shape=(jax.ShapeDtypeStruct(linear, F32), jax.ShapeDtypeStruct(linear, F32)),
+        in_specs=[hbm] * 14,
         out_specs=(hbm, hbm),
         scratch_shapes=[
-            pltpu.VMEM((NV, OWN, 1024), F32),
-            pltpu.VMEM((NV, OWN, 1024), F32),
-            pltpu.VMEM((NV, OWN, 1024), F32),
+            pltpu.VMEM((1, 1024), F32),
+            pltpu.VMEM((1, 256), F32),
+            pltpu.VMEM((1, 256), F32),
+            pltpu.VMEM((1, 256), jnp.int32),
+            pltpu.VMEM((1, 256), jnp.int32),
+            pltpu.SMEM((NH,), jnp.int32),
+            pltpu.VMEM(deriv.shape, BF16),
+            pltpu.VMEM(a.shape, F32),
+            pltpu.VMEM(f.shape, F32),
+            pltpu.VMEM(order.shape, jnp.int32),
+            pltpu.VMEM(own, F32),
+            pltpu.VMEM(own, F32),
+            pltpu.VMEM(own, F32),
             pltpu.VMEM((OWN, 25, 1024), BF16),
             pltpu.VMEM((OWN, 25, 1024), BF16),
             pltpu.VMEM((OWN, 32, 1024), BF16),
+            pltpu.VMEM((NV * NV * ROWS, OWN * 32), BF16),
             pltpu.VMEM((25, ROWS, 1024), F32),
             pltpu.VMEM((25, ROWS, 1024), F32),
+            pltpu.VMEM(field, F32),
             pltpu.VMEM(field, F32),
             pltpu.VMEM(field, F32),
             pltpu.VMEM(field, F32),
@@ -310,22 +368,29 @@
             pltpu.VMEM((4, FR, 256), F32),
             pltpu.VMEM((2, NV, ROWS, 256), F32),
             pltpu.VMEM((2,) + field, F32),
-            pltpu.VMEM((NV, OWN, 1024), F32),
-            pltpu.VMEM((NV, OWN, 1024), F32),
-            pltpu.SemaphoreType.DMA((4,)),
-            pltpu.SemaphoreType.DMA((2,)),
-            pltpu.SemaphoreType.DMA((6,)),
-            pltpu.SemaphoreType.DMA((6,)),
+            pltpu.VMEM(own, F32),
+            pltpu.VMEM(own, F32),
+            pltpu.SemaphoreType.DMA((12,)),
+            pltpu.SemaphoreType.DMA((8,)),
+            pltpu.SemaphoreType.DMA((8,)),
+            pltpu.SemaphoreType.DMA((8,)),
+            pltpu.SemaphoreType.DMA((8,)),
+            pltpu.SemaphoreType.DMA((8,)),
+            pltpu.SemaphoreType.DMA((8,)),
+            pltpu.SemaphoreType.DMA((5,)),
+            pltpu.SemaphoreType.DMA((5,)),
         ],
         compiler_params=pltpu.CompilerParams(
-            collective_id=0, has_side_effects=True, vmem_limit_bytes=48 * 1024 * 1024
+            collective_id=0, has_side_effects=True, vmem_limit_bytes=VMEM_LIMIT
         ),
         name="harmonic_blade_row",
     )(
-        tangent_seed, adjoint_seed, jacobian, precond, upwind, up_weight, bottom_face_strength,
+        tangent_seed.reshape(linear), adjoint_seed.reshape(linear), jacobian, precond,
+        upwind, up_weight, bottom_face_strength,
         up_cells.reshape(1, -1), lo_cells.reshape(1, -1), phase_index,
-        deriv, a, f, order, perm,
+        deriv, a, f, order,
     )
+    return (tangent_out.reshape(tangent_seed.shape), adjoint_out.reshape(adjoint_seed.shape))
 
 
 def solution(mesh):

time: 24.5 us -> 20.7 us (0.84)
  local copies, waits for them, and re-layouts: 7.88 us -> 2.39 us
  Pallas kernels: 15.5 us -> 17.5 us
    unnamed x28 -> x4, local copies, waits for them, and re-layouts: 5.98 us -> 2.39 us
    pallas_call x1, Pallas kernels: 15.5 us -> 17.5 us  [on_device(): pl.pallas_call(functools.partial(kernel, passages), out_shape=(jax.ShapeD...]
    pallas_call x2 -> x0, local copies, waits for them, and re-layouts: 1.89 us -> none  [on_device(): pl.pallas_call(functools.partial(kernel, passages), out_shape=(jax.ShapeD...]
where the time goes in v2:
time: 20.7 us; the launch traced here: 20.5 us
  Pallas kernels  17.5 us (85%)
  local copies, waits for them, and re-layouts  2.39 us (12%)
  between operations  0.65 us (3%)
    pallas_call x1, Pallas kernels, on_device(): pl.pallas_call(functools.partial(kernel, passages), out_shape=(jax.ShapeD...  17.5 us
    unnamed x4, local copies, waits for them, and re-layouts  2.39 us

profile of v2, /device:TPU:0, one launch (start us, length us, event | category | flops | bytes accessed | tf_op | source)
XLA Modules:
  0.0 20.5 jit_solution(7827555544129616471)
XLA Ops:
  0.6 17.5 %harmonic_blade_row.1 = (f32[5,12,8,1,128]{4,3,2,1,0:T(1,128)}, f32[5,12,8,1,128]{4,3,2,1,0:T(1,128)}) custom-call(f32[5,12,8,1,128]{4,3,2,1,0:T(1,128)} %bitcast.6, f32[5,12,8,1,128]{4,3,2,1,0:T(1,128)} %bitcast.7, bf16[1,12,25,1024]{3,2,1,0:T(8,128)(2,1)} %jac_hbm.1, bf16[1,12,25,1024]{3,2,1,0:T(8,128)(2,1)} %pre_hbm.1, f32[1,1024]{1,0:T(1,128)} %upwind_hbm.1, ...), custom_call_target="tpu_custom_call" | custom-call | tf_op jit(solution)/shard_map/harmonic_blade_row/pallas_call | solution.py:335
  18.1 0.0 copy-start
  18.2 1.7 %copy.20 = f32[1,5,12,1024]{3,0,2,1:T(1,128)} copy(f32[1,5,12,1024]{3,0,2,1:T(1,128)} %bitcast.9) | data formatting | bytes 491520
  19.8 0.0 copy-done
  19.9 0.7 %copy.21 = f32[1,5,12,1024]{3,0,2,1:T(1,128)} copy(f32[1,5,12,1024]{3,0,2,1:T(1,128)S(1)} %bitcast.8) | data formatting | bytes 491520
Async XLA Ops:
  18.1 1.7 %copy-start = (f32[5,12,8,1,128]{4,3,2,1,0:T(1,128)S(1)}, f32[5,12,8,1,128]{4,3,2,1,0:T(1,128)}, u32[]{:S(2)}) copy-start(f32[5,12,8,1,128]{4,3,2,1,0:T(1,128)} %get-tuple-element.5) | copy-start | bytes 737284

commit v3 on v2

--- a/solution.py
+++ b/solution.py
@@ -95,11 +95,11 @@
     passages,
     tan_hbm, adj_hbm, jac_hbm, pre_hbm, upwind_hbm, upw_hbm, bot_hbm, up_hbm, lo_hbm, phase_hbm,
     deriv_hbm, a_hbm, f_hbm, order_hbm,
-    tan_out, adj_out,
+    tan_stage, adj_stage,
     upwind_ref, upw_ref, bot_ref, up_ref, lo_ref, phase_ref, deriv_ref, a_ref, f_ref, order_ref,
     tan_own, adj_own, tan_far, jac, pre, mpad, perm, jt, pt,
-    vt, vd, va, vfar, dual_far, sel_lo, sel_up, send, recv, spread, img, tan_stage, adj_stage,
-    in_sem, tan_sem, adj_sem, tan_out_sem, adj_out_sem, far_send, far_recv, send_sem, recv_sem,
+    vt, vd, va, vfar, dual_far, sel_lo, sel_up, send, recv, spread, img,
+    in_sem, tan_sem, adj_sem, far_send, far_recv, send_sem, recv_sem,
 ):
     blade, inst = lax.axis_index("blade"), lax.axis_index("inst")
     ring = lax.axis_size("blade")
@@ -295,30 +295,31 @@
             total = (total[:VR] + total[VR:]).reshape(NV, ROWS, 512)
             img[base // 2, :, :, cells] = img[base // 2, :, :, cells] - total
 
-    def stores(src, dst, sems):
-        return [
-            pltpu.make_async_copy(src.at[:, :, chunk(n)], dst.at[:, :, n, 0, :], sems.at[n])
-            for n in range(8)
-        ]
-
-    tan_stores = stores(tan_stage, tan_out, tan_out_sem)
-    adj_stores = stores(adj_stage, adj_out, adj_out_sem)
-
     for copy in face_sends[:2]:
         copy.wait()
     add_faces(0, (upw_ref, bot_ref))
     for n in range(8):
         for i in range(NV):
             tan_stage[i, :, chunk(n)] = block(pt, img.at[0], i, chunk(n), False)[:OWN]
-        tan_stores[n].start()
 
     for copy in face_sends[2:]:
         copy.wait()
     add_faces(2, None)
     for n in range(8):
         adj_stage[:, :, chunk(n)] = img[1, :, 0:OWN, chunk(n)]
-        adj_stores[n].start()
-    for copy in tan_stores + adj_stores:
+
+
+def finish(tan_ref, adj_ref, tan_out, adj_out, sems):
+    stores = [
+        pltpu.make_async_copy(
+            src.at[:, :, 128 * n : 128 * n + 128], dst.at[:, :, n, 0, :], sems.at[m, n]
+        )
+        for m, (src, dst) in enumerate(((tan_ref, tan_out), (adj_ref, adj_out)))
+        for n in range(8)
+    ]
+    for copy in stores:
+        copy.start()
+    for copy in stores:
         copy.wait()
 
 
@@ -331,12 +332,13 @@
     own = (NV, OWN, 1024)
     field = (NV, ROWS, 1024)
     linear = (NV, OWN, 8, 1, 128)
-    hbm = pl.BlockSpec(memory_space=pl.ANY)
-    tangent_out, adjoint_out = pl.pallas_call(
+    hbm = pl.BlockSpec(memory_space=pltpu.HBM)
+    vmem = pl.BlockSpec(memory_space=pltpu.VMEM)
+    staged = pl.pallas_call(
         functools.partial(kernel, passages),
-        out_shape=(jax.ShapeDtypeStruct(linear, F32), jax.ShapeDtypeStruct(linear, F32)),
+        out_shape=(pltpu.VMEM(own, F32), pltpu.VMEM(own, F32)),
         in_specs=[hbm] * 14,
-        out_specs=(hbm, hbm),
+        out_specs=(vmem, vmem),
         scratch_shapes=[
             pltpu.VMEM((1, 1024), F32),
             pltpu.VMEM((1, 256), F32),
@@ -368,11 +370,7 @@
             pltpu.VMEM((4, FR, 256), F32),
             pltpu.VMEM((2, NV, ROWS, 256), F32),
             pltpu.VMEM((2,) + field, F32),
-            pltpu.VMEM(own, F32),
-            pltpu.VMEM(own, F32),
             pltpu.SemaphoreType.DMA((12,)),
-            pltpu.SemaphoreType.DMA((8,)),
-            pltpu.SemaphoreType.DMA((8,)),
             pltpu.SemaphoreType.DMA((8,)),
             pltpu.SemaphoreType.DMA((8,)),
             pltpu.SemaphoreType.DMA((8,)),
@@ -390,6 +388,15 @@
         up_cells.reshape(1, -1), lo_cells.reshape(1, -1), phase_index,
         deriv, a, f, order,
     )
+    tangent_out, adjoint_out = pl.pallas_call(
+        finish,
+        out_shape=(jax.ShapeDtypeStruct(linear, F32), jax.ShapeDtypeStruct(linear, F32)),
+        in_specs=[vmem, vmem],
+        out_specs=(hbm, hbm),
+        scratch_shapes=[pltpu.SemaphoreType.DMA((2, 8))],
+        compiler_params=pltpu.CompilerParams(vmem_limit_bytes=4 * 1024 * 1024),
+        name="finish",
+    )(*staged)
     return (tangent_out.reshape(tangent_seed.shape), adjoint_out.reshape(adjoint_seed.shape))
 
 

time: 20.7 us -> 18.4 us (0.89)
  local copies, waits for them, and re-layouts: 2.39 us -> 0 us
    unnamed x4 -> x0, local copies, waits for them, and re-layouts: 2.39 us -> none
    pallas_call x1 -> x2, Pallas kernels: 17.5 us -> 17.6 us  [the longest x1 16.7 us: on_device(): pl.pallas_call(functools.partial(kernel, passages), out_shape=(pltpu.VMEM...]
where the time goes in v3:
time: 18.4 us; the launch traced here: 18.2 us
  Pallas kernels  17.6 us (96%)
  between operations  0.64 us (3%)
    pallas_call x1, Pallas kernels, on_device(): pl.pallas_call(functools.partial(kernel, passages), out_shape=(pltpu.VMEM...  16.7 us
    pallas_call x1, Pallas kernels, on_device(): pl.pallas_call(finish, out_shape=(jax.ShapeDtypeStruct(linear, F32), jax....  0.9 us

profile of v3, /device:TPU:0, one launch (start us, length us, event | category | flops | bytes accessed | tf_op | source)
XLA Modules:
  0.0 18.2 jit_solution(17802128812343771120)
XLA Ops:
  0.6 16.7 %harmonic_blade_row.1 = (f32[5,12,1024]{2,1,0:T(8,128)S(1)}, f32[5,12,1024]{2,1,0:T(8,128)S(1)}) custom-call(f32[5,12,8,1,128]{4,3,2,1,0:T(1,128)} %bitcast.6, f32[5,12,8,1,128]{4,3,2,1,0:T(1,128)} %bitcast.7, bf16[1,12,25,1024]{3,2,1,0:T(8,128)(2,1)} %jac_hbm.1, bf16[1,12,25,1024]{3,2,1,0:T(8,128)(2,1)} %pre_hbm.1, f32[1,1024]{1,0:T(1,128)} %upwind_hbm.1, ...), custom_call_target="tpu_custom_call" | custom-call | tf_op jit(solution)/shard_map/harmonic_blade_row/pallas_call | solution.py:337
  17.3 0.9 %finish.1 = (f32[5,12,8,1,128]{4,3,2,1,0:T(1,128)}, f32[5,12,8,1,128]{4,3,2,1,0:T(1,128)}) custom-call(f32[5,12,1024]{2,1,0:T(8,128)S(1)} %get-tuple-element.6.tan_ref, f32[5,12,1024]{2,1,0:T(8,128)S(1)} %get-tuple-element.7.adj_ref), custom_call_target="tpu_custom_call" | custom-call | tf_op jit(solution)/shard_map/finish/pallas_call | solution.py:391
